TPU v7x, 256 devices: a whole 4x4x8 slice. The times are simulated.
256 devices in a mesh: ctx: 32 (over z, y_hi, core), kv: 8 (over x, y_lo).
Axes of the slice: x: 4, y: 4 (y_hi: 2, y_lo: 2; y = y_hi * 2 + y_lo), z: 8, core: 2. Of those that a mesh axis runs over, the one named last changes fastest.
Arguments:
- queries: bfloat16 [1024, 64, 128], P('ctx', 'kv'), may hold values from -64 to 64
- new_keys: bfloat16 [1024, 8, 128], P('ctx', 'kv'), may hold values from -8 to 8
- new_values: bfloat16 [1024, 8, 128], P('ctx', 'kv'), may hold values from -6 to 6
- key_cache: bfloat16 [262144, 8, 128], P('ctx', 'kv'), may hold values from -6 to 6
- value_cache: bfloat16 [262144, 8, 128], P('ctx', 'kv'), may hold values from -6 to 6
- page_slots: int32 [32, 32, 8], P('ctx'), may hold values from 0 to 63, as said below
- page_counts: int32 [32, 32], P('ctx'), may hold values from 0 to 8, as said below
- out_weight: bfloat16 [8192, 8192], P('kv', 'ctx'), may hold values from -1.5 to 1.5
Outputs:
- layer_out: bfloat16 [1024, 8192], P('kv', 'ctx')
Inputs may be any that keep to these rules, and one draw needn't show every extreme that they name: page_counts[s, b] of the 8 slots of page_slots[s, b] hold selected pages; for every block b some shard s has exactly 8. The 8 entries of page_slots[s, b] are distinct pages of shard s; only the first page_counts[s, b] are selected, the others are not read.
All inputs are finite; a program needn't handle non-finite values.
Results may differ from a plain program's by a relative error of at most 0.019.
Values may be sent and summed in bfloat16 or wider, within the bound.
A program may use at most 64 MiB of HBM per device.

v0:
```python
import jax
import jax.numpy as jnp
from jax import lax
from jax.sharding import PartitionSpec as P

PAGE = 128


NEG_FILL = -1e30


def from_behind(value, axis, steps):
    count = lax.axis_size(axis)
    pairs = [(source, (source + steps) % count) for source in range(count)]
    return lax.ppermute(value, axis, pairs)


def masked_part(query_rows, key_rows, value_rows, live_mask, factor):
    scores = (
        jnp.einsum("tkgd,nkd->tkgn", query_rows, key_rows, preferred_element_type=jnp.float32)
        * factor
    )
    widened = live_mask[:, None, None, :]
    highest = jnp.max(jnp.where(widened, scores, NEG_FILL), axis=-1)
    weights = jnp.where(widened, jnp.exp(scores - highest[..., None]), 0.0).astype(jnp.bfloat16)
    totals = jnp.sum(weights, axis=-1, dtype=jnp.float32)
    summed = jnp.einsum("tkgn,nkd->tkgd", weights, value_rows, preferred_element_type=jnp.float32)
    return (summed, highest, totals)


def body(
    queries, new_keys, new_values, key_cache, value_cache, page_slots, page_counts, out_weight
):
    q_len = queries.shape[0]
    heads_local = queries.shape[1]
    width = queries.shape[2]
    kv_local = new_keys.shape[1]
    group = heads_local // kv_local
    shards = lax.axis_size("ctx")
    my_block = lax.axis_index("ctx")
    factor = width ** (-0.5)
    local_pages = key_cache.shape[0] // PAGE
    key_pages = key_cache.reshape(local_pages, PAGE, kv_local, width)
    value_pages = value_cache.reshape(local_pages, PAGE, kv_local, width)
    slot_table = page_slots[0]
    count_table = page_counts[0]

    def block_part(q_block, block_index):
        query_rows = q_block.reshape(q_len, kv_local, group, width)
        page_list = slot_table[block_index]
        live_count = count_table[block_index]
        key_rows = jnp.take(key_pages, page_list, axis=0).reshape(-1, kv_local, width)
        value_rows = jnp.take(value_pages, page_list, axis=0).reshape(-1, kv_local, width)
        live_pages = jnp.arange(page_list.shape[0], dtype=jnp.int32) < live_count
        live_mask = jnp.broadcast_to(
            jnp.repeat(live_pages, PAGE)[None, :], (q_len, key_rows.shape[0])
        )
        result = masked_part(query_rows, key_rows, value_rows, live_mask, factor)
        return result

    all_new_keys, all_new_values = (
        lax.all_gather(new_keys, "ctx", axis=0, tiled=True),
        lax.all_gather(new_values, "ctx", axis=0, tiled=True),
    )
    query_pos = my_block * q_len + jnp.arange(q_len, dtype=jnp.int32)
    key_pos = jnp.arange(all_new_keys.shape[0], dtype=jnp.int32)
    causal = key_pos[None, :] <= query_pos[:, None]
    new_sum, new_top, new_total = masked_part(
        queries.reshape(q_len, kv_local, group, width), all_new_keys, all_new_values, causal, factor
    )
    own_parts = block_part(queries, my_block)
    holders = tuple(
        (
            lax.dynamic_update_index_in_dim(
                jnp.zeros((shards,) + piece_out.shape, jnp.float32), piece_out, my_block, 0
            )
            for piece_out in own_parts
        )
    )

    def visit(turn, carry):
        visitor, held = carry
        visitor = from_behind(visitor, "ctx", 1)
        owner = jnp.mod(my_block - turn, shards)
        fresh_parts = block_part(visitor, owner)
        held = tuple(
            (
                lax.dynamic_update_index_in_dim(holder, piece_out, owner, 0)
                for holder, piece_out in zip(held, fresh_parts)
            )
        )
        return (visitor, held)

    carried = lax.fori_loop(1, shards, visit, (queries, holders))
    part_sums, part_tops, part_totals = carried[1]
    got_sums, got_tops, got_totals = (
        lax.all_to_all(part_sums, "ctx", split_axis=0, concat_axis=0, tiled=True),
        lax.all_to_all(part_tops, "ctx", split_axis=0, concat_axis=0, tiled=True),
        lax.all_to_all(part_totals, "ctx", split_axis=0, concat_axis=0, tiled=True),
    )
    highest = jnp.maximum(jnp.max(got_tops, axis=0), new_top)
    cache_scale = jnp.exp(got_tops - highest[None])
    summed = jnp.sum(got_sums * cache_scale[..., None], axis=0)
    totals = jnp.sum(got_totals * cache_scale, axis=0)
    new_scale = jnp.exp(new_top - highest)
    summed = summed + new_sum * new_scale[..., None]
    totals = totals + new_total * new_scale
    attention = (
        (summed / totals[..., None]).astype(jnp.bfloat16).reshape(q_len, heads_local * width)
    )
    context = lax.all_gather(attention, "ctx", axis=0, tiled=True)
    return lax.psum_scatter(
        jnp.dot(context, out_weight, preferred_element_type=jnp.float32).astype(jnp.bfloat16),
        "kv",
        scatter_dimension=0,
        tiled=True,
    )


def solution(mesh):
    placed = (
        P("ctx", "kv", None),
        P("ctx", "kv", None),
        P("ctx", "kv", None),
        P("ctx", "kv", None),
        P("ctx", "kv", None),
        P("ctx", None, None),
        P("ctx", None),
        P("kv", "ctx"),
    )
    return jax.shard_map(
        body, mesh=mesh, in_specs=placed, out_specs=P("kv", "ctx"), check_vma=False
    )
```

profile of v0, /device:TPU:5, one launch (start us, length us, event | category | flops | bytes accessed | tf_op | source)
XLA Modules:
  0.0 632.9 jit_solution(14265389743891642876)
XLA Ops:
  20.2 285.8 %while.21 = (s32[]{:T(128)}, bf16[32,8,128]{2,0,1:T(8,128)(2,1)S(1)}, f32[32,32,1,8,128]{4,1,3,2,0:T(8,128)}, f32[32,32,1,8]{1,3,2,0:T(8,128)S(1)}, f32[32,32,1,...) while((s32[]{:T(128)}, ...), condition=%wide.region_5.7_spmd, body=%wide.region_2.6_spmd.sunk | while | flops 137364032 | bytes 6386212 | solution.py:94
  20.2 3.5 collective-permute-start
  23.7 2.2 gather_fusion
  25.9 2.2 gather_fusion.1
  33.7 2.2 gather_fusion.1
  41.1 2.2 gather_fusion
  43.3 2.2 gather_fusion.1
  51.3 2.2 gather_fusion.1
  56.8 3.3 collective-permute-start
  60.1 2.2 gather_fusion
  62.3 2.2 gather_fusion.1
  93.1 3.2 collective-permute-start
  129.5 3.2 collective-permute-start
  148.5 2.9 collective-permute-start
  306.7 8.6 %all-to-all-start.1 = ((f32[32,1,256]{2,1,0:T(1,128)}), f32[32,1,256]{2,1,0:T(1,128)S(1)}, u32[]{:S(2)}, u32[]{:S(2)}) async-start(f32[32,1,256]{2,1,0:T(1,128)} %reshape.308), calls=%async_computation.1 | async-start | bytes 65536 | tf_op jit(solution)/shard_map/all_to_all | solution.py:98
  315.4 9.5 %all-to-all-done.1 = f32[32,1,256]{2,1,0:T(1,128)S(1)} async-done(((f32[32,1,256]{2,1,0:T(1,128)}), f32[32,1,256]{2,1,0:T(1,128)S(1)}, u32[]{:S(2)}, u32[]{:S(2)}) %all-to-all-start.1) | async-done | bytes 32800 | tf_op jit(solution)/shard_map/all_to_all | solution.py:98
  324.9 12.8 %all_to_all.15 = f32[32,1,256]{2,1,0:T(1,128)S(1)} all-to-all(f32[32,1,256]{2,1,0:T(1,128)S(1)} %reshape.310), channel_id=1, replica_groups=mesh['ctx'=32,'kv'=8] {'ctx'}, dimensions={0} | all-to-all | bytes 65536 | tf_op jit(solution)/shard_map/all_to_all | solution.py:99
  337.7 5.0 all-to-all-start
  342.7 125.0 %all_gather.9 = bf16[1024,1,128]{2,0,1:T(8,128)(2,1)S(1)} all-gather(bf16[32,1,128]{2,0,1:T(8,128)(2,1)S(1)} %copy-done.3), channel_id=1, replica_groups=mesh['ctx'=32,'kv'=8] {'ctx'}, dimensions={0}, use_global_device_ids=true | all-gather | bytes 270336 | tf_op jit(solution)/shard_map/all_gather | solution.py:62
  467.7 40.2 %all_gather.10 = bf16[1024,1,128]{2,0,1:T(8,128)(2,1)S(1)} all-gather(bf16[32,1,128]{2,0,1:T(8,128)(2,1)S(1)} %copy-done.4), channel_id=1, replica_groups=mesh['ctx'=32,'kv'=8] {'ctx'}, dimensions={0}, use_global_device_ids=true | all-gather | bytes 270336 | tf_op jit(solution)/shard_map/all_gather | solution.py:63
  511.1 2.8 multiply_reduce_fusion
  515.0 79.7 %all-gather.2.cloned.1.call-done = bf16[1024,1024]{1,0:T(8,128)(2,1)} async-done(((bf16[32,1024]{1,0:T(8,128)(2,1)}), bf16[1024,1024]{1,0:T(8,128)(2,1)}) %all-gather.2.cloned.1.call-update) | async-done | bytes 2097168 | tf_op jit(solution)/shard_map/all_gather | solution.py:111
  594.7 3.1 convolution_convert_fusion
  597.8 28.2 %reduce-scatter.2.cloned.1.call-done = bf16[128,256]{1,0:T(8,128)(2,1)} async-done(((bf16[1024,256]{1,0:T(8,128)(2,1)}), bf16[128,256]{1,0:T(8,128)(2,1)}) %reduce-scatter.2.cloned.1.call-update) | async-done | bytes 65552 | tf_op jit(solution)/shard_map/reduce_scatter | solution.py:112
  (507 shorter events, 268.7 us)
Async XLA Ops:
  20.2 9.5 %collective-permute-start = (bf16[32,8,128]{2,0,1:T(8,128)(2,1)S(1)}, bf16[32,8,128]{2,0,1:T(8,128)(2,1)S(1)}, u32[]{:S(2)}, u32[]{:S(2)}) collective-permute-start(bf16[32,8,128]{2,0,1:T(8,128)(2,1)S(1)} %get-tuple-element.424), channel_id=1, source_target_pairs={{0,8},{8,16},{16,24},{24,32},{32,40},{40,48},{48,56},{56,64},{64,7... | collective-permute-start | bytes 196616 | tf_op jit(solution)/shard_map/while/body/eval_jaxpr/ppermute | solution.py:15
  39.3 7.8 %collective-permute-start = (bf16[32,8,128]{2,0,1:T(8,128)(2,1)S(1)}, bf16[32,8,128]{2,0,1:T(8,128)(2,1)S(1)}, u32[]{:S(2)}, u32[]{:S(2)}) collective-permute-start(bf16[32,8,128]{2,0,1:T(8,128)(2,1)S(1)} %get-tuple-element.424), channel_id=1, source_target_pairs={{0,8},{8,16},{16,24},{24,32},{32,40},{40,48},{48,56},{56,64},{64,7... | collective-permute-start | bytes 196616 | tf_op jit(solution)/shard_map/while/body/eval_jaxpr/ppermute | solution.py:15
  56.8 9.2 %collective-permute-start = (bf16[32,8,128]{2,0,1:T(8,128)(2,1)S(1)}, bf16[32,8,128]{2,0,1:T(8,128)(2,1)S(1)}, u32[]{:S(2)}, u32[]{:S(2)}) collective-permute-start(bf16[32,8,128]{2,0,1:T(8,128)(2,1)S(1)} %get-tuple-element.424), channel_id=1, source_target_pairs={{0,8},{8,16},{16,24},{24,32},{32,40},{40,48},{48,56},{56,64},{64,7... | collective-permute-start | bytes 196616 | tf_op jit(solution)/shard_map/while/body/eval_jaxpr/ppermute | solution.py:15
  75.7 7.7 %collective-permute-start = (bf16[32,8,128]{2,0,1:T(8,128)(2,1)S(1)}, bf16[32,8,128]{2,0,1:T(8,128)(2,1)S(1)}, u32[]{:S(2)}, u32[]{:S(2)}) collective-permute-start(bf16[32,8,128]{2,0,1:T(8,128)(2,1)S(1)} %get-tuple-element.424), channel_id=1, source_target_pairs={{0,8},{8,16},{16,24},{24,32},{32,40},{40,48},{48,56},{56,64},{64,7... | collective-permute-start | bytes 196616 | tf_op jit(solution)/shard_map/while/body/eval_jaxpr/ppermute | solution.py:15
  93.1 9.2 %collective-permute-start = (bf16[32,8,128]{2,0,1:T(8,128)(2,1)S(1)}, bf16[32,8,128]{2,0,1:T(8,128)(2,1)S(1)}, u32[]{:S(2)}, u32[]{:S(2)}) collective-permute-start(bf16[32,8,128]{2,0,1:T(8,128)(2,1)S(1)} %get-tuple-element.424), channel_id=1, source_target_pairs={{0,8},{8,16},{16,24},{24,32},{32,40},{40,48},{48,56},{56,64},{64,7... | collective-permute-start | bytes 196616 | tf_op jit(solution)/shard_map/while/body/eval_jaxpr/ppermute | solution.py:15
  112.1 7.8 %collective-permute-start = (bf16[32,8,128]{2,0,1:T(8,128)(2,1)S(1)}, bf16[32,8,128]{2,0,1:T(8,128)(2,1)S(1)}, u32[]{:S(2)}, u32[]{:S(2)}) collective-permute-start(bf16[32,8,128]{2,0,1:T(8,128)(2,1)S(1)} %get-tuple-element.424), channel_id=1, source_target_pairs={{0,8},{8,16},{16,24},{24,32},{32,40},{40,48},{48,56},{56,64},{64,7... | collective-permute-start | bytes 196616 | tf_op jit(solution)/shard_map/while/body/eval_jaxpr/ppermute | solution.py:15
  129.5 9.2 %collective-permute-start = (bf16[32,8,128]{2,0,1:T(8,128)(2,1)S(1)}, bf16[32,8,128]{2,0,1:T(8,128)(2,1)S(1)}, u32[]{:S(2)}, u32[]{:S(2)}) collective-permute-start(bf16[32,8,128]{2,0,1:T(8,128)(2,1)S(1)} %get-tuple-element.424), channel_id=1, source_target_pairs={{0,8},{8,16},{16,24},{24,32},{32,40},{40,48},{48,56},{56,64},{64,7... | collective-permute-start | bytes 196616 | tf_op jit(solution)/shard_map/while/body/eval_jaxpr/ppermute | solution.py:15
  148.5 8.9 %collective-permute-start = (bf16[32,8,128]{2,0,1:T(8,128)(2,1)S(1)}, bf16[32,8,128]{2,0,1:T(8,128)(2,1)S(1)}, u32[]{:S(2)}, u32[]{:S(2)}) collective-permute-start(bf16[32,8,128]{2,0,1:T(8,128)(2,1)S(1)} %get-tuple-element.424), channel_id=1, source_target_pairs={{0,8},{8,16},{16,24},{24,32},{32,40},{40,48},{48,56},{56,64},{64,7... | collective-permute-start | bytes 196616 | tf_op jit(solution)/shard_map/while/body/eval_jaxpr/ppermute | solution.py:15
  159.1 7.4 %collective-permute-start = (bf16[32,8,128]{2,0,1:T(8,128)(2,1)S(1)}, bf16[32,8,128]{2,0,1:T(8,128)(2,1)S(1)}, u32[]{:S(2)}, u32[]{:S(2)}) collective-permute-start(bf16[32,8,128]{2,0,1:T(8,128)(2,1)S(1)} %get-tuple-element.424), channel_id=1, source_target_pairs={{0,8},{8,16},{16,24},{24,32},{32,40},{40,48},{48,56},{56,64},{64,7... | collective-permute-start | bytes 196616 | tf_op jit(solution)/shard_map/while/body/eval_jaxpr/ppermute | solution.py:15
  168.3 8.0 %collective-permute-start = (bf16[32,8,128]{2,0,1:T(8,128)(2,1)S(1)}, bf16[32,8,128]{2,0,1:T(8,128)(2,1)S(1)}, u32[]{:S(2)}, u32[]{:S(2)}) collective-permute-start(bf16[32,8,128]{2,0,1:T(8,128)(2,1)S(1)} %get-tuple-element.424), channel_id=1, source_target_pairs={{0,8},{8,16},{16,24},{24,32},{32,40},{40,48},{48,56},{56,64},{64,7... | collective-permute-start | bytes 196616 | tf_op jit(solution)/shard_map/while/body/eval_jaxpr/ppermute | solution.py:15
  178.1 7.4 %collective-permute-start = (bf16[32,8,128]{2,0,1:T(8,128)(2,1)S(1)}, bf16[32,8,128]{2,0,1:T(8,128)(2,1)S(1)}, u32[]{:S(2)}, u32[]{:S(2)}) collective-permute-start(bf16[32,8,128]{2,0,1:T(8,128)(2,1)S(1)} %get-tuple-element.424), channel_id=1, source_target_pairs={{0,8},{8,16},{16,24},{24,32},{32,40},{40,48},{48,56},{56,64},{64,7... | collective-permute-start | bytes 196616 | tf_op jit(solution)/shard_map/while/body/eval_jaxpr/ppermute | solution.py:15
  196.3 7.4 %collective-permute-start = (bf16[32,8,128]{2,0,1:T(8,128)(2,1)S(1)}, bf16[32,8,128]{2,0,1:T(8,128)(2,1)S(1)}, u32[]{:S(2)}, u32[]{:S(2)}) collective-permute-start(bf16[32,8,128]{2,0,1:T(8,128)(2,1)S(1)} %get-tuple-element.424), channel_id=1, source_target_pairs={{0,8},{8,16},{16,24},{24,32},{32,40},{40,48},{48,56},{56,64},{64,7... | collective-permute-start | bytes 196616 | tf_op jit(solution)/shard_map/while/body/eval_jaxpr/ppermute | solution.py:15
  205.5 7.3 %collective-permute-start = (bf16[32,8,128]{2,0,1:T(8,128)(2,1)S(1)}, bf16[32,8,128]{2,0,1:T(8,128)(2,1)S(1)}, u32[]{:S(2)}, u32[]{:S(2)}) collective-permute-start(bf16[32,8,128]{2,0,1:T(8,128)(2,1)S(1)} %get-tuple-element.424), channel_id=1, source_target_pairs={{0,8},{8,16},{16,24},{24,32},{32,40},{40,48},{48,56},{56,64},{64,7... | collective-permute-start | bytes 196616 | tf_op jit(solution)/shard_map/while/body/eval_jaxpr/ppermute | solution.py:15
  214.6 7.5 %collective-permute-start = (bf16[32,8,128]{2,0,1:T(8,128)(2,1)S(1)}, bf16[32,8,128]{2,0,1:T(8,128)(2,1)S(1)}, u32[]{:S(2)}, u32[]{:S(2)}) collective-permute-start(bf16[32,8,128]{2,0,1:T(8,128)(2,1)S(1)} %get-tuple-element.424), channel_id=1, source_target_pairs={{0,8},{8,16},{16,24},{24,32},{32,40},{40,48},{48,56},{56,64},{64,7... | collective-permute-start | bytes 196616 | tf_op jit(solution)/shard_map/while/body/eval_jaxpr/ppermute | solution.py:15
  232.9 7.4 %collective-permute-start = (bf16[32,8,128]{2,0,1:T(8,128)(2,1)S(1)}, bf16[32,8,128]{2,0,1:T(8,128)(2,1)S(1)}, u32[]{:S(2)}, u32[]{:S(2)}) collective-permute-start(bf16[32,8,128]{2,0,1:T(8,128)(2,1)S(1)} %get-tuple-element.424), channel_id=1, source_target_pairs={{0,8},{8,16},{16,24},{24,32},{32,40},{40,48},{48,56},{56,64},{64,7... | collective-permute-start | bytes 196616 | tf_op jit(solution)/shard_map/while/body/eval_jaxpr/ppermute | solution.py:15
  242.1 7.4 %collective-permute-start = (bf16[32,8,128]{2,0,1:T(8,128)(2,1)S(1)}, bf16[32,8,128]{2,0,1:T(8,128)(2,1)S(1)}, u32[]{:S(2)}, u32[]{:S(2)}) collective-permute-start(bf16[32,8,128]{2,0,1:T(8,128)(2,1)S(1)} %get-tuple-element.424), channel_id=1, source_target_pairs={{0,8},{8,16},{16,24},{24,32},{32,40},{40,48},{48,56},{56,64},{64,7... | collective-permute-start | bytes 196616 | tf_op jit(solution)/shard_map/while/body/eval_jaxpr/ppermute | solution.py:15
  251.2 7.4 %collective-permute-start = (bf16[32,8,128]{2,0,1:T(8,128)(2,1)S(1)}, bf16[32,8,128]{2,0,1:T(8,128)(2,1)S(1)}, u32[]{:S(2)}, u32[]{:S(2)}) collective-permute-start(bf16[32,8,128]{2,0,1:T(8,128)(2,1)S(1)} %get-tuple-element.424), channel_id=1, source_target_pairs={{0,8},{8,16},{16,24},{24,32},{32,40},{40,48},{48,56},{56,64},{64,7... | collective-permute-start | bytes 196616 | tf_op jit(solution)/shard_map/while/body/eval_jaxpr/ppermute | solution.py:15
  260.3 7.3 %collective-permute-start = (bf16[32,8,128]{2,0,1:T(8,128)(2,1)S(1)}, bf16[32,8,128]{2,0,1:T(8,128)(2,1)S(1)}, u32[]{:S(2)}, u32[]{:S(2)}) collective-permute-start(bf16[32,8,128]{2,0,1:T(8,128)(2,1)S(1)} %get-tuple-element.424), channel_id=1, source_target_pairs={{0,8},{8,16},{16,24},{24,32},{32,40},{40,48},{48,56},{56,64},{64,7... | collective-permute-start | bytes 196616 | tf_op jit(solution)/shard_map/while/body/eval_jaxpr/ppermute | solution.py:15
  269.4 7.4 %collective-permute-start = (bf16[32,8,128]{2,0,1:T(8,128)(2,1)S(1)}, bf16[32,8,128]{2,0,1:T(8,128)(2,1)S(1)}, u32[]{:S(2)}, u32[]{:S(2)}) collective-permute-start(bf16[32,8,128]{2,0,1:T(8,128)(2,1)S(1)} %get-tuple-element.424), channel_id=1, source_target_pairs={{0,8},{8,16},{16,24},{24,32},{32,40},{40,48},{48,56},{56,64},{64,7... | collective-permute-start | bytes 196616 | tf_op jit(solution)/shard_map/while/body/eval_jaxpr/ppermute | solution.py:15
  287.7 7.4 %collective-permute-start = (bf16[32,8,128]{2,0,1:T(8,128)(2,1)S(1)}, bf16[32,8,128]{2,0,1:T(8,128)(2,1)S(1)}, u32[]{:S(2)}, u32[]{:S(2)}) collective-permute-start(bf16[32,8,128]{2,0,1:T(8,128)(2,1)S(1)} %get-tuple-element.424), channel_id=1, source_target_pairs={{0,8},{8,16},{16,24},{24,32},{32,40},{40,48},{48,56},{56,64},{64,7... | collective-permute-start | bytes 196616 | tf_op jit(solution)/shard_map/while/body/eval_jaxpr/ppermute | solution.py:15
  306.7 18.2 %all-to-all-start.1 = ((f32[32,1,256]{2,1,0:T(1,128)}), f32[32,1,256]{2,1,0:T(1,128)S(1)}, u32[]{:S(2)}, u32[]{:S(2)}) async-start(f32[32,1,256]{2,1,0:T(1,128)} %reshape.308), calls=%async_computation.1 | async-start | bytes 65536 | tf_op jit(solution)/shard_map/all_to_all | solution.py:98
  337.7 173.4 %all-to-all-start = ((f32[32,32,1,8,128]{4,1,3,2,0:T(8,128)}), f32[32,32,1,8,128]{4,1,3,2,0:T(8,128)}, u32[]{:S(2)}, u32[]{:S(2)}) async-start(f32[32,32,1,8,128]{4,1,3,2,0:T(8,128)} %get-tuple-element.251), calls=%async_computation | async-start | bytes 8388608 | tf_op jit(solution)/shard_map/all_to_all | solution.py:97
  342.7 252.1 %all-gather.2.cloned.1.call-start = ((), (), s32[]{:S(2)}) async-start(), calls=%async_computation.4 | async-start | bytes 2162688 | tf_op jit(solution)/shard_map/all_gather | solution.py:111
  515.0 111.0 %reduce-scatter.2.cloned.1.call-start = ((), (), s32[]{:S(2)}) async-start(), calls=%async_computation.5 | async-start | bytes 589824 | tf_op jit(solution)/shard_map/reduce_scatter | solution.py:112
  (17 other events, 972.8 us)
Sparse Core Ops, SparseCore 0:
  515.1 79.5 all-gather.1
  598.0 28.0 reduce-scatter.1
where the time goes:
time: 644 us; the launch traced here: 633 us
  blocking collectives  178 us (28%)
  local copies, waits for them, and re-layouts  172 us (27%)
  waiting for transfers between devices  117 us (18%)
  starting transfers between devices  59.5 us (9%)
  matrix products  48.3 us (8%)
  other arithmetic  41.9 us (7%)
  between operations  13.7 us (2%)
    all_gather x1, blocking collectives, body(): lax.all_gather(new_keys, 'ctx', axis=0, tiled=True)  125 us
    all_gather x1, waiting for transfers between devices, body(): context = lax.all_gather(attention, 'ctx', axis=0, tiled=True)  79.7 us
    gather x32, local copies, waits for them, and re-layouts, block_part(): jnp.take(key_pages, page_list, axis=0).reshape(-1, kv_local, width)  70.1 us
    gather x32, local copies, waits for them, and re-layouts, block_part(): jnp.take(value_pages, page_list, axis=0).reshape(-1, kv_local, width)  70.1 us
    ppermute x31, starting transfers between devices, from_behind(): return lax.ppermute(value, axis, pairs)  45.9 us
    all_gather x1, blocking collectives, body(): lax.all_gather(new_values, 'ctx', axis=0, tiled=True)  40.2 us
    dot_general x33, matrix products, masked_part(): jnp.einsum('tkgn,nkd->tkgd', weights, value_rows, preferred_element_type=...  31.9 us
    reduce_scatter x1, waiting for transfers between devices, body(): lax.psum_scatter(jnp.dot(context, out_weight, preferred_element_type=jnp....  28.2 us
  transfers between devices with their start and end apart: 35, of which 3 were waited for; matrix products, arithmetic and copies ran while one was open for 30% of the time, Pallas kernels for 0%

commit v1 on v0

v1 whole, which is shorter than its diff:
```python
import jax
import jax.numpy as jnp
from jax import lax
from jax.experimental import pallas as pl
from jax.experimental.pallas import tpu as pltpu
from jax.sharding import PartitionSpec as P

PAGE = 128
HEAD = 128
ROWS = 256
MSG = 144
QTOK = 32
ZS = 8
BLOCKS = 32
NEG_FILL = -1e30
LOG2E = 1.4426950408889634
FACTOR = HEAD ** (-0.5) * LOG2E
MIB = 1 << 20
MESH = pl.DeviceIdType.MESH

LEN = ((4, 3), (3, 4))
WAYS = (1, -1)


class Place:
    def __init__(self):
        self.me = lax.axis_index("ctx")
        self.kv = lax.axis_index("kv")
        self.z = self.me // 4
        self.yh = (self.me % 4) // 2
        self.core = self.me % 2

    def block(self, dz, chain, other_core=False):
        z = lax.rem(self.z + dz + ZS, ZS)
        yh = 1 - self.yh if chain else self.yh
        core = 1 - self.core if other_core else self.core
        return z * 4 + yh * 2 + core


def remote(src, dst, send, recv, ctx):
    return pltpu.make_async_remote_copy(
        src_ref=src, dst_ref=dst, send_sem=send, recv_sem=recv,
        device_id={"ctx": ctx}, device_id_type=MESH,
    )


def greet(place, with_kv):
    barrier = pltpu.get_barrier_semaphore()
    peers = (place.block(1, 0), place.block(-1, 0), place.block(0, 1), place.block(0, 0, True))
    for peer in peers:
        pl.semaphore_signal(barrier, inc=1, device_id={"ctx": peer}, device_id_type=MESH)
    count = len(peers)
    if with_kv:
        for off in range(1, ZS):
            other = lax.rem(place.kv + off, ZS)
            pl.semaphore_signal(barrier, inc=1, device_id={"kv": other}, device_id_type=MESH)
        count += ZS - 1
    pl.semaphore_wait(barrier, count)


def pair_slot(dz, chain):
    return (dz % ZS) * 2 + chain


def gather_blocks(place, slots, zsend, zrecv, csend, crecv, ysem, planes=None):
    started = []

    def send_z(dz, chain, way, step):
        b = place.block(dz, chain)
        copy = remote(
            slots.at[b], slots.at[b], zsend.at[chain, way, step - 1], zrecv.at[chain, way, step - 1],
            place.block(WAYS[way], 0),
        )
        copy.start()
        started.append(copy)

    def send_core(dz, chain):
        b = place.block(dz, chain)
        k = pair_slot(dz, chain)
        copy = remote(slots.at[b], slots.at[b], csend.at[k], crecv.at[k], place.block(0, 0, True))
        copy.start()
        started.append(copy)

    def wait_core(dz, chain):
        b = place.block(dz, chain, True)
        k = pair_slot(dz, chain)
        remote(slots.at[b], slots.at[b], csend.at[k], crecv.at[k], place.block(0, 0, True)).wait_recv()

    def plane(dz):
        for chain in (0, 1):
            wait_core(dz, chain)
        if planes is not None:
            planes(dz)

    own = place.block(0, 0)
    partner = place.block(0, 1)
    y_copy = remote(slots.at[own], slots.at[own], ysem.at[0], ysem.at[1], partner)
    y_copy.start()
    started.append(y_copy)
    send_z(0, 0, 0, 1)
    send_z(0, 0, 1, 1)
    send_core(0, 0)
    remote(slots.at[partner], slots.at[partner], ysem.at[0], ysem.at[1], partner).wait_recv()
    send_z(0, 1, 0, 1)
    send_z(0, 1, 1, 1)
    send_core(0, 1)
    for step in range(1, 5):
        for chain in (0, 1):
            for way in (0, 1):
                if LEN[chain][way] < step:
                    continue
                dz = -step * WAYS[way]
                b = place.block(dz, chain)
                remote(
                    slots.at[b], slots.at[b], zsend.at[chain, way, step - 1], zrecv.at[chain, way, step - 1],
                    place.block(WAYS[way], 0),
                ).wait_recv()
                if step < LEN[chain][way]:
                    send_z(dz, chain, way, step + 1)
                send_core(dz, chain)
        if step == 1:
            plane(0)
        else:
            plane(step - 1)
            plane(1 - step)
    plane(4)
    for copy in started:
        copy.wait_send()


GATHER_SEMS = [
    pltpu.SemaphoreType.DMA((2, 2, 4)),
    pltpu.SemaphoreType.DMA((2, 2, 4)),
    pltpu.SemaphoreType.DMA((16,)),
    pltpu.SemaphoreType.DMA((16,)),
    pltpu.SemaphoreType.DMA((2,)),
]


def gather_kernel(q_ref, v_ref, nv_ref, g_ref, vt_ref, nvt_ref, *sems):
    place = Place()
    greet(place, False)
    g_ref[place.me] = q_ref[...]

    def turn(i, _):
        at = pl.multiple_of(i * PAGE, PAGE)
        vt_ref[i, 0:HEAD, :] = v_ref[pl.ds(at, PAGE), :].T
        vt_ref[i, HEAD:MSG, :] = jnp.ones((MSG - HEAD, PAGE), jnp.bfloat16)
        return 0

    count = v_ref.shape[0] // PAGE
    lax.fori_loop(0, count, turn, 0)
    nvt_ref[0:HEAD, :] = nv_ref[...].T
    nvt_ref[HEAD:MSG, :] = jnp.ones((MSG - HEAD, QTOK), jnp.bfloat16)
    gather_blocks(place, g_ref, *sems)


def gather_queries(q, v, nv):
    pages = v.shape[0] // PAGE
    return pl.pallas_call(
        gather_kernel,
        out_shape=(
            jax.ShapeDtypeStruct((BLOCKS, ROWS, HEAD), jnp.bfloat16),
            jax.ShapeDtypeStruct((pages, MSG, PAGE), jnp.bfloat16),
            jax.ShapeDtypeStruct((MSG, QTOK), jnp.bfloat16),
        ),
        in_specs=[pl.BlockSpec(memory_space=pltpu.VMEM)] * 3,
        out_specs=[pl.BlockSpec(memory_space=pltpu.VMEM)] * 3,
        scratch_shapes=GATHER_SEMS,
        compiler_params=pltpu.CompilerParams(
            collective_id=0, has_side_effects=True, vmem_limit_bytes=20 * MIB
        ),
        name="gather_queries",
    )(q, v, nv)


def write_message(ref, top, total, sums):
    ref[0:HEAD, :] = sums.astype(jnp.bfloat16)
    high = total.astype(jnp.bfloat16).astype(jnp.float32)
    low = total - high
    row = lax.broadcasted_iota(jnp.int32, (MSG - HEAD, ROWS), 0)
    stats = jnp.where(row == 0, top, jnp.where(row == 1, high, jnp.where(row == 2, low, 0.0)))
    ref[HEAD:MSG, :] = stats.astype(jnp.bfloat16)


def merged(refs):
    tops, totals = [], []
    for ref in refs:
        stats = ref[HEAD:MSG, :].astype(jnp.float32)
        tops.append(stats[0:1, :])
        totals.append(stats[1:2, :] + stats[2:3, :])
    top = tops[0]
    for other in tops[1:]:
        top = jnp.maximum(top, other)
    total = None
    sums = None
    for ref, t, n in zip(refs, tops, totals):
        scale = jnp.exp2(t - top)
        piece = ref[0:HEAD, :].astype(jnp.float32) * scale
        total = n * scale if total is None else total + n * scale
        sums = piece if sums is None else sums + piece
    return top, total, sums


def partial_kernel(slots_ref, counts_ref, q_ref, k_ref, vt_ref, nk_ref, nvt_ref, out_ref):
    shard = lax.axis_index("ctx")
    contract = (((1,), (1,)), ((), ()))

    def one(b, _):
        count = counts_ref[b]

        def case(n):
            def run():
                q = q_ref[b]
                new = lax.dot_general(nk_ref[...], q, contract, preferred_element_type=jnp.float32)
                key = lax.broadcasted_iota(jnp.int32, (QTOK, ROWS), 0)
                token = lax.broadcasted_iota(jnp.int32, (QTOK, ROWS), 1) // (ROWS // QTOK)
                live = key + shard * QTOK <= token + b * QTOK
                new = jnp.where(live, new, NEG_FILL)
                scores = []
                pages = []
                top = jnp.max(new, axis=0, keepdims=True)
                for j in range(n):
                    page = slots_ref[b, j]
                    pages.append(page)
                    at = pl.multiple_of(page * PAGE, PAGE)
                    scores.append(
                        lax.dot_general(
                            k_ref[pl.ds(at, PAGE), :], q, contract, preferred_element_type=jnp.float32
                        )
                    )
                if n:
                    most = scores[0]
                    for other in scores[1:]:
                        most = jnp.maximum(most, other)
                    top = jnp.maximum(top, jnp.max(most, axis=0, keepdims=True))
                top = jnp.maximum(top * FACTOR, NEG_FILL).astype(jnp.bfloat16).astype(jnp.float32)
                weights = jnp.where(live, jnp.exp2(new * FACTOR - top), 0.0).astype(jnp.bfloat16)
                both = jnp.dot(nvt_ref[...], weights, preferred_element_type=jnp.float32)
                if n:
                    weights = [jnp.exp2(s * FACTOR - top).astype(jnp.bfloat16) for s in scores]
                    values = [vt_ref[page] for page in pages]
                    both = both + jnp.dot(
                        jnp.concatenate(values, axis=1) if n > 1 else values[0],
                        jnp.concatenate(weights, axis=0) if n > 1 else weights[0],
                        preferred_element_type=jnp.float32,
                    )
                write_message(out_ref.at[b], top, both[HEAD : HEAD + 1, :], both[0:HEAD, :])

            return run

        for n in range(9):
            pl.when(count == n)(case(n))
        return 0

    lax.fori_loop(0, BLOCKS, one, 0)


def partials(slots, counts, q, k, vt, nk, nvt):
    return pl.pallas_call(
        partial_kernel,
        out_shape=jax.ShapeDtypeStruct((BLOCKS, MSG, ROWS), jnp.bfloat16),
        in_specs=[pl.BlockSpec(memory_space=pltpu.SMEM)] * 2 + [pl.BlockSpec(memory_space=pltpu.VMEM)] * 5,
        out_specs=pl.BlockSpec(memory_space=pltpu.VMEM),
        compiler_params=pltpu.CompilerParams(vmem_limit_bytes=24 * MIB),
        name="partials",
    )(slots, counts, q, k, vt, nk, nvt)


def finish_kernel(
    p_ref, w_ref, out_ref,
    c_buf, t_buf, r_buf, y_buf, turned, a_buf, mine_buf, kv_buf,
    c_send, c_recv, z_send, z_recv, y_sem, kv_send, kv_recv, *sems,
):
    place = Place()
    greet(place, True)
    started = []
    sibling = place.block(0, 0, True)

    order = [(dz, chain) for far in (4, 3, 2, 1) for dz in ((far, -far) if far < 4 else (4,)) for chain in (0, 1)]
    order += [(0, 1), (0, 0)]
    for dz, chain in order:
        k = pair_slot(dz, chain)
        copy = remote(p_ref.at[place.block(dz, chain, True)], c_buf.at[k], c_send.at[k], c_recv.at[k], sibling)
        copy.start()
        started.append(copy)

    def local(dz, chain):
        k = pair_slot(dz, chain)
        b = place.block(dz, chain)
        remote(p_ref.at[b], c_buf.at[k], c_send.at[k], c_recv.at[k], sibling).wait_recv()
        return [p_ref.at[b], c_buf.at[k]]

    def z_copy(chain, way, step):
        at = chain, way, step - 1
        return remote(t_buf.at[at], r_buf.at[at], z_send.at[at], z_recv.at[at], place.block(WAYS[way], 0))

    for step in range(1, 5):
        for chain in (0, 1):
            for way in (0, 1):
                length = LEN[chain][1 - way]
                if step > length:
                    continue
                parts = local(WAYS[way] * (length + 1 - step), chain)
                if step > 1:
                    z_copy(chain, way, step - 1).wait_recv()
                    parts.append(r_buf.at[chain, way, step - 2])
                write_message(t_buf.at[chain, way, step - 1], *merged(parts))
                copy = z_copy(chain, way, step)
                copy.start()
                started.append(copy)

    def home(chain):
        parts = local(0, chain)
        for way in (0, 1):
            length = LEN[chain][1 - way]
            z_copy(chain, way, length).wait_recv()
            parts.append(r_buf.at[chain, way, length - 1])
        return parts

    write_message(y_buf.at[0], *merged(home(1)))
    y_copy = remote(y_buf.at[0], y_buf.at[1], y_sem.at[0], y_sem.at[1], place.block(0, 1))
    y_copy.start()
    parts = home(0)
    y_copy.wait()
    _, total, sums = merged(parts + [y_buf.at[1]])
    turned[...] = (sums * (1.0 / total)).T
    heads = ROWS // QTOK
    for g in range(heads):
        a_buf[place.me, :, g * HEAD : (g + 1) * HEAD] = turned[pl.ds(g, QTOK, stride=heads), :].astype(jnp.bfloat16)

    def kv_copy(target, step):
        return pltpu.make_async_remote_copy(
            src_ref=mine_buf.at[target], dst_ref=kv_buf.at[place.kv],
            send_sem=kv_send.at[target], recv_sem=kv_recv.at[place.kv],
            device_id={"kv": target}, device_id_type=MESH,
        )

    def project(dz):
        plane = lax.rem(place.z + dz + ZS, ZS)
        rows = a_buf[pl.ds(pl.multiple_of(plane * 4, 4), 4)].reshape(4 * QTOK, a_buf.shape[2])
        mine_buf[plane] = jnp.dot(rows, w_ref[...], preferred_element_type=jnp.float32).astype(jnp.bfloat16)

        @pl.when(plane != place.kv)
        def _():
            kv_copy(plane, dz).start()

    gather_blocks(place, a_buf, *sems, planes=project)

    total = mine_buf[place.kv].astype(jnp.float32)
    for off in range(1, ZS):
        other = lax.rem(place.kv + off, ZS)
        pltpu.make_async_remote_copy(
            src_ref=mine_buf.at[other], dst_ref=kv_buf.at[other],
            send_sem=kv_send.at[other], recv_sem=kv_recv.at[other],
            device_id={"kv": other}, device_id_type=MESH,
        ).wait()
        total = total + kv_buf[other].astype(jnp.float32)
    out_ref[...] = total.astype(jnp.bfloat16)
    for copy in started:
        copy.wait_send()


def finish(p, w):
    width = w.shape[1]
    return pl.pallas_call(
        finish_kernel,
        out_shape=jax.ShapeDtypeStruct((4 * QTOK, width), jnp.bfloat16),
        in_specs=[pl.BlockSpec(memory_space=pltpu.VMEM)] * 2,
        out_specs=pl.BlockSpec(memory_space=pltpu.VMEM),
        scratch_shapes=[
            pltpu.VMEM((16, MSG, ROWS), jnp.bfloat16),
            pltpu.VMEM((2, 2, 4, MSG, ROWS), jnp.bfloat16),
            pltpu.VMEM((2, 2, 4, MSG, ROWS), jnp.bfloat16),
            pltpu.VMEM((2, MSG, ROWS), jnp.bfloat16),
            pltpu.VMEM((ROWS, HEAD), jnp.float32),
            pltpu.VMEM((BLOCKS, QTOK, w.shape[0]), jnp.bfloat16),
            pltpu.VMEM((ZS, 4 * QTOK, width), jnp.bfloat16),
            pltpu.VMEM((ZS, 4 * QTOK, width), jnp.bfloat16),
            pltpu.SemaphoreType.DMA((16,)),
            pltpu.SemaphoreType.DMA((16,)),
            pltpu.SemaphoreType.DMA((2, 2, 4)),
            pltpu.SemaphoreType.DMA((2, 2, 4)),
            pltpu.SemaphoreType.DMA((2,)),
            pltpu.SemaphoreType.DMA((ZS,)),
            pltpu.SemaphoreType.DMA((ZS,)),
        ]
        + GATHER_SEMS,
        compiler_params=pltpu.CompilerParams(
            collective_id=1, has_side_effects=True, vmem_limit_bytes=24 * MIB
        ),
        name="finish",
    )(p, w)


def body(queries, new_keys, new_values, key_cache, value_cache, page_slots, page_counts, out_weight):
    q = queries.reshape(ROWS, HEAD)
    nk = new_keys.reshape(QTOK, HEAD)
    nv = new_values.reshape(QTOK, HEAD)
    k = key_cache.reshape(-1, HEAD)
    v = value_cache.reshape(-1, HEAD)
    g, vt, nvt = gather_queries(q, v, nv)
    p = partials(page_slots[0], page_counts[0], g, k, vt, nk, nvt)
    return finish(p, out_weight)


def solution(mesh):
    placed = (
        P("ctx", "kv", None),
        P("ctx", "kv", None),
        P("ctx", "kv", None),
        P("ctx", "kv", None),
        P("ctx", "kv", None),
        P("ctx", None, None),
        P("ctx", None),
        P("kv", "ctx"),
    )
    return jax.shard_map(
        body, mesh=mesh, in_specs=placed, out_specs=P("kv", "ctx"), check_vma=False
    )
```

time: 644 us -> 108 us (0.17); the launches traced: 633 us -> 108 us
  blocking collectives: 178 us -> 0 us
  local copies, waits for them, and re-layouts: 172 us -> 4.69 us
  waiting for transfers between devices: 117 us -> 0 us
  Pallas kernels: 0 us -> 103 us
  starting transfers between devices: 59.5 us -> 0 us
  matrix products: 48.3 us -> 0 us
  other arithmetic: 41.9 us -> 0 us
  between operations: 13.7 us -> 0.07 us
    all_gather x2 -> x0, blocking collectives: 165 us -> none  [the longest x1 125 us: body(): lax.all_gather(new_keys, 'ctx', axis=0, tiled=True)]
    gather x64 -> x0, local copies, waits for them, and re-layouts: 140 us -> none  [the longest x32 70.1 us: block_part(): jnp.take(key_pages, page_list, axis=0).reshape(-1, kv_local, width)]
    pallas_call x0 -> x3, Pallas kernels: none -> 103 us  [the longest x1 52.8 us: finish(): pl.pallas_call(finish_kernel, out_shape=jax.ShapeDtypeStruct((4 * QTOK, w...]
    all_gather x1 -> x0, waiting for transfers between devices: 79.7 us -> none  [body(): context = lax.all_gather(attention, 'ctx', axis=0, tiled=True)]
    dot_general x67 -> x0, matrix products: 48.3 us -> none  [the longest x33 31.9 us: masked_part(): jnp.einsum('tkgn,nkd->tkgd', weights, value_rows, preferred_element_type=...]
    ppermute x31 -> x0, starting transfers between devices: 45.9 us -> none  [from_behind(): return lax.ppermute(value, axis, pairs)]
    reduce_scatter x1 -> x0, waiting for transfers between devices: 28.2 us -> none  [body(): lax.psum_scatter(jnp.dot(context, out_weight, preferred_element_type=jnp....]
    dynamic_slice x33 -> x0, local copies, waits for them, and re-layouts: 23 us -> none  [the longest x32 22.1 us: block_part(): live_count = count_table[block_index]]
  transfers between devices with their start and end apart: 35 -> 0, of which waited for: 3 -> 0; matrix products, arithmetic and copies ran while one was open for 30% -> 0% of each run, Pallas kernels for 0% -> 0%
where the time goes in v1:
time: 108 us
  Pallas kernels  103 us (95%)
  local copies, waits for them, and re-layouts  4.69 us (4%)
    pallas_call x1, Pallas kernels, finish(): pl.pallas_call(finish_kernel, out_shape=jax.ShapeDtypeStruct((4 * QTOK, w...  52.8 us
    pallas_call x1, Pallas kernels, gather_queries(): pl.pallas_call(gather_kernel, out_shape=(jax.ShapeDtypeStruct((BLOCKS, RO...  32.4 us
    pallas_call x1, Pallas kernels, partials(): pl.pallas_call(partial_kernel, out_shape=jax.ShapeDtypeStruct((BLOCKS, MS...  18.2 us
    unnamed x16, local copies, waits for them, and re-layouts  4.69 us

profile of v1, /device:TPU:5, one launch (start us, length us, event | category | flops | bytes accessed | tf_op | source)
XLA Modules:
  0.0 108.2 jit_solution(9371142192177429266)
XLA Ops:
  0.0 0.0 copy-start
  0.0 0.9 copy.9
  0.9 0.0 copy-start.1
  0.9 1.6 %copy-done.1 = bf16[8192,1,128]{2,0,1:T(8,128)(2,1)S(1)} copy-done((bf16[8192,1,128]{2,0,1:T(8,128)(2,1)S(1)}, bf16[8192,1,128]{2,0,1:T(8,128)(2,1)}, u32[]{:S(2)}) %copy-start.1) | copy-done | bytes 2097176
  2.5 0.0 copy-start.3
  2.5 0.8 copy-done.3
  3.3 0.0 copy-start.4
  3.3 0.7 copy-done.4
  4.0 0.0 copy-start.5
  4.0 0.0 copy-start.6
  4.0 32.4 %gather_queries.1 = (bf16[32,256,128]{2,1,0:T(8,128)(2,1)S(1)}, bf16[64,144,128]{2,1,0:T(8,128)(2,1)S(1)}, bf16[144,32]{1,0:T(8,128)(2,1)S(1)}) custom-call(bf16[256,128]{1,0:T(8,128)(2,1)S(1)} %bitcast.10, bf16[8192,128]{1,0:T(8,128)(2,1)S(1)} %bitcast.8, bf16[32,128]{1,0:T(8,128)(2,1)S(1)} %bitcast.11), custom_call_target="tpu_custom_call" | custom-call | tf_op jit(solution)/shard_map/gather_queries/pallas_call | solution.py:160
  36.5 0.0 copy-done
  36.5 0.0 copy-done.5
  36.5 0.0 copy-done.6
  36.5 0.0 copy-start.2
  36.5 18.2 %partials.1.p_ref = bf16[32,144,256]{2,1,0:T(8,128)(2,1)S(1)} custom-call(s32[32,8]{1,0:T(8,128)S(1)} %bitcast.9, s32[32]{0:T(128)S(1)} %bitcast.13, bf16[32,256,128]{2,1,0:T(8,128)(2,1)S(1)} %get-tuple-element.8.q_ref, bf16[8192,128]{1,0:T(8,128)(2,1)S(1)} %bitcast.7, bf16[64,144,128]{2,1,0:T(8,128)(2,1)S(1)} %get-tuple-element.9.vt_ref, ...), custom_call_target="tpu_custom_call" | custom-call | tf_op jit(solution)/shard_map/partials/pallas_call | solution.py:260
  54.7 0.0 copy-done.2
  54.7 52.8 %finish.1 = bf16[128,256]{1,0:T(8,128)(2,1)S(1)} custom-call(bf16[32,144,256]{2,1,0:T(8,128)(2,1)S(1)} %partials.1.p_ref, bf16[1024,256]{1,0:T(8,128)(2,1)S(1)} %copy-done.2), custom_call_target="tpu_custom_call" | custom-call | tf_op jit(solution)/shard_map/finish/pallas_call | solution.py:366
  107.5 0.6 copy.11
Async XLA Ops:
  0.0 36.5 %copy-start = (bf16[8192,1,128]{2,0,1:T(8,128)(2,1)S(1)}, bf16[8192,1,128]{2,0,1:T(8,128)(2,1)}, u32[]{:S(2)}) copy-start(bf16[8192,1,128]{2,0,1:T(8,128)(2,1)} %param.11) | copy-start | bytes 6291460
  0.9 1.6 %copy-start.1 = (bf16[8192,1,128]{2,0,1:T(8,128)(2,1)S(1)}, bf16[8192,1,128]{2,0,1:T(8,128)(2,1)}, u32[]{:S(2)}) copy-start(bf16[8192,1,128]{2,0,1:T(8,128)(2,1)} %param.12) | copy-start | bytes 6291460
  2.5 0.8 copy-start.3
  3.3 0.7 copy-start.4
  4.0 32.5 %copy-start.5 = (bf16[32,1,128]{2,0,1:T(8,128)(2,1)S(1)}, bf16[32,1,128]{2,0,1:T(8,128)(2,1)}, u32[]{:S(2)}) copy-start(bf16[32,1,128]{2,0,1:T(8,128)(2,1)} %param.9) | copy-start | bytes 24580
  4.0 32.5 %copy-start.6 = (s32[1,32]{1,0:T(1,128)S(1)}, s32[1,32]{1,0:T(1,128)}, u32[]{:S(2)}) copy-start(s32[1,32]{1,0:T(1,128)} %param.14) | copy-start | bytes 388
  36.5 18.2 %copy-start.2 = (bf16[1024,256]{1,0:T(8,128)(2,1)S(1)}, bf16[1024,256]{1,0:T(8,128)(2,1)}, u32[]{:S(2)}) copy-start(bf16[1024,256]{1,0:T(8,128)(2,1)} %w_ref.1) | copy-start | bytes 1572868

commit v2 on v0

v2 whole, which is shorter than its diff:
```python
import jax
import jax.numpy as jnp
from jax import lax
from jax.experimental import pallas as pl
from jax.experimental.pallas import tpu as pltpu
from jax.sharding import PartitionSpec as P

PAGE = 128
HEAD = 128
QTOK = 32
GROUP = 8
HALF = 128
MSG = 144
ZS = 8
COLUMN = 16
MOST = 8
NEG_FILL = -1e30
FACTOR = HEAD ** (-0.5) * 1.4426950408889634
MIB = 1 << 20
MESH = pl.DeviceIdType.MESH
BF16 = jnp.bfloat16
F32 = jnp.float32

LEN = ((4, 3), (3, 4))
WAYS = (1, -1)
HALVES = (0, 1)


class Place:
    def __init__(self):
        self.me = lax.axis_index("ctx")
        self.kv = lax.axis_index("kv")
        self.z = self.me // 4
        self.yh = (self.me % 4) // 2
        self.core = self.me % 2
        self.above = self.block(1, 0)
        self.below = self.block(-1, 0)
        self.partner = self.block(0, 1)
        self.sibling = self.z * 4 + self.yh * 2 + 1 - self.core

    def slot(self, dz, chain):
        z = lax.rem(self.z + dz + ZS, ZS)
        return z * 2 + (1 - self.yh if chain else self.yh)

    def block(self, dz, chain):
        return self.slot(dz, chain) * 2 + self.core

    def along(self, way):
        return self.below if way else self.above


def remote(src, dst, send, recv, **where):
    return pltpu.make_async_remote_copy(
        src_ref=src, dst_ref=dst, send_sem=send, recv_sem=recv, device_id=where, device_id_type=MESH
    )


def greet(wheres):
    barrier = pltpu.get_barrier_semaphore()
    for where in wheres:
        pl.semaphore_signal(barrier, inc=1, device_id=where, device_id_type=MESH)
    pl.semaphore_wait(barrier, len(wheres))


class Gather:
    def __init__(self, place, slots, own, z_send, z_recv, y_send, y_recv):
        self.place, self.slots, self.own = place, slots, own
        self.sems = z_send, z_recv, y_send, y_recv
        self.started = []

    def z_copy(self, chain, way, step, half, src=None):
        here = self.slots.at[self.place.slot(-(step - 1) * WAYS[way], chain), half]
        at = chain, way, step - 1, half
        return remote(
            here if src is None else src, here, self.sems[0].at[at], self.sems[1].at[at], ctx=self.place.along(way)
        )

    def z_start(self, *args, **more):
        copy = self.z_copy(*args, **more)
        copy.start()
        self.started.append(copy)

    def z_wait(self, chain, way, step, half):
        there = self.slots.at[self.place.slot(-step * WAYS[way], chain), half]
        at = chain, way, step - 1, half
        remote(there, there, self.sems[0].at[at], self.sems[1].at[at], ctx=self.place.along(way)).wait_recv()

    def start(self, half):
        src = self.own(half)
        copy = remote(
            src, self.slots.at[self.place.slot(0, 0), half], self.sems[2].at[half], self.sems[3].at[half],
            ctx=self.place.partner,
        )
        copy.start()
        self.started.append(copy)
        for way in (0, 1):
            self.z_start(0, way, 1, half, src=src)

    def partner(self):
        for half in HALVES:
            there = self.slots.at[self.place.slot(0, 1), half]
            remote(
                there, there, self.sems[2].at[half], self.sems[3].at[half], ctx=self.place.partner
            ).wait_recv()
            for way in (0, 1):
                self.z_start(1, way, 1, half)

    def hop(self, chain, step, between=None):
        for half in HALVES:
            for way in (0, 1):
                if LEN[chain][way] < step:
                    continue
                if between is not None:
                    between()
                self.z_wait(chain, way, step, half)
                if step < LEN[chain][way]:
                    self.z_start(chain, way, step + 1, half)

    def finish(self):
        for copy in self.started:
            copy.wait_send()


GATHER_SEMS = [
    pltpu.SemaphoreType.DMA((2, 2, 4, 2)),
    pltpu.SemaphoreType.DMA((2, 2, 4, 2)),
    pltpu.SemaphoreType.DMA((2,)),
    pltpu.SemaphoreType.DMA((2,)),
]


def exchange_kernel(
    q_ref, k_ref, v_ref, nk_ref, nv_ref, slots_ref, counts_ref, w_ref,
    g_out, k_out, vt_out, new_out, slots_out, counts_out, w_out,
    v_buf, l_sem, c_send, c_recv, *sems,
):
    place = Place()
    pages = v_buf.shape[0]
    local = [
        pltpu.make_async_copy(src, dst, l_sem.at[i])
        for i, (src, dst) in enumerate(
            (
                (v_ref, v_buf),
                (k_ref, k_out.at[0]),
                (q_ref, g_out.at[place.slot(0, 0)]),
                (nk_ref, new_out.at[0, 0]),
                (nv_ref, new_out.at[0, 1]),
                (slots_ref, slots_out.at[0]),
                (counts_ref, counts_out.at[0]),
                (w_ref, w_out.at[0]),
            )
        )
    ]
    for copy in local:
        copy.start()
    greet([dict(ctx=where) for where in (place.above, place.below, place.partner, place.sibling)])

    gather = Gather(place, g_out, lambda half: q_ref.at[half], *sems)
    for half in HALVES:
        gather.start(half)

    to_sibling = []

    def give(src, dst):
        i = len(to_sibling)
        copy = remote(src, dst, c_send.at[i], c_recv.at[i], ctx=place.sibling)
        copy.start()
        to_sibling.append(copy)

    give(slots_ref, slots_out.at[1])
    give(counts_ref, counts_out.at[1])
    give(nk_ref, new_out.at[1, 0])
    give(nv_ref, new_out.at[1, 1])
    quarter = pages // 4
    for i in range(4):
        part = pl.ds(i * quarter, quarter)
        give(k_ref.at[part], k_out.at[1, part])
    give(w_ref, w_out.at[1])

    todo = list(range(16))
    each = pages // 16

    def between():
        if not todo:
            return
        i = todo.pop(0)
        if i == 0:
            local[0].wait()

        def turn(p, _):
            vt_out[0, p, 0:HEAD, :] = v_buf[p].T
            vt_out[0, p, HEAD:MSG, :] = jnp.ones((MSG - HEAD, PAGE), BF16)
            vt_out[1, p, HEAD:MSG, :] = jnp.ones((MSG - HEAD, PAGE), BF16)
            return 0

        lax.fori_loop(i * each, (i + 1) * each, turn, 0)
        if i % 4 == 3:
            part = pl.ds((i - 3) * each, 4 * each), pl.ds(0, HEAD)
            give(vt_out.at[(0,) + part], vt_out.at[(1,) + part])

    gather.hop(0, 1, between)
    gather.partner()
    gather.hop(0, 2, between)
    gather.hop(1, 1, between)
    gather.hop(0, 3, between)
    gather.hop(1, 2, between)
    while todo:
        between()
    gather.hop(0, 4)
    gather.hop(1, 3)
    gather.hop(1, 4)
    gather.finish()
    for copy in local[1:]:
        copy.wait()
    for copy in to_sibling:
        copy.wait()


def exchange(q, k, v, nk, nv, slots, counts, w):
    pages = v.shape[0]
    n_give = 13
    return pl.pallas_call(
        exchange_kernel,
        out_shape=(
            jax.ShapeDtypeStruct((COLUMN, 2, HALF, HEAD), BF16),
            jax.ShapeDtypeStruct((2, pages, PAGE, HEAD), BF16),
            jax.ShapeDtypeStruct((2, pages, MSG, PAGE), BF16),
            jax.ShapeDtypeStruct((2, 2, QTOK, HEAD), BF16),
            jax.ShapeDtypeStruct((2,) + slots.shape, jnp.int32),
            jax.ShapeDtypeStruct((2,) + counts.shape, jnp.int32),
            jax.ShapeDtypeStruct((2,) + w.shape, BF16),
        ),
        in_specs=[pl.BlockSpec(memory_space=pltpu.HBM)] * 8,
        out_specs=[pl.BlockSpec(memory_space=pltpu.VMEM)] * 7,
        scratch_shapes=[
            pltpu.VMEM((pages, PAGE, HEAD), BF16),
            pltpu.SemaphoreType.DMA((8,)),
            pltpu.SemaphoreType.DMA((n_give,)),
            pltpu.SemaphoreType.DMA((n_give,)),
        ]
        + GATHER_SEMS,
        compiler_params=pltpu.CompilerParams(
            collective_id=0, has_side_effects=True, vmem_limit_bytes=24 * MIB
        ),
        name="exchange",
    )(q, k, v, nk, nv, slots, counts, w)


def write_message(ref, top, total, sums):
    ref[0:HEAD, :] = sums.astype(BF16)
    high = total.astype(BF16).astype(F32)
    low = total - high
    row = lax.broadcasted_iota(jnp.int32, (MSG - HEAD, HALF), 0)
    stats = jnp.where(row == 0, top, jnp.where(row == 1, high, jnp.where(row == 2, low, 0.0)))
    ref[HEAD:MSG, :] = stats.astype(BF16)


def merged(refs):
    tops, totals = [], []
    for ref in refs:
        stats = ref[HEAD:MSG, :].astype(F32)
        tops.append(stats[0:1, :])
        totals.append(stats[1:2, :] + stats[2:3, :])
    top = tops[0]
    for other in tops[1:]:
        top = jnp.maximum(top, other)
    total = None
    sums = None
    for ref, t, n in zip(refs, tops, totals):
        scale = jnp.exp2(t - top)
        piece = ref[0:HEAD, :].astype(F32) * scale
        total = n * scale if total is None else total + n * scale
        sums = piece if sums is None else sums + piece
    return top, total, sums


def partial_kernel(slots_ref, counts_ref, q_ref, k_ref, vt_ref, new_ref, out_ref, nvt, earlier):
    me = lax.axis_index("ctx")
    core = me % 2
    pages = k_ref.shape[1]
    contract = (((1,), (1,)), ((), ()))
    fresh = 2 * QTOK
    rows = 2 * HALF
    nvt[0:HEAD, :] = new_ref[:, 1].reshape(fresh, HEAD).astype(F32).T.astype(BF16)
    nvt[HEAD:MSG, :] = jnp.ones((MSG - HEAD, fresh), BF16)

    def block_of(slot):
        return slot * 2 + core

    def attend(slot, n, start):
        b = block_of(slot)
        own = counts_ref[0, 0, b]
        live_pages = own + counts_ref[1, 0, b] - start
        q = q_ref[slot].reshape(rows, HEAD)
        new = lax.dot_general(new_ref[:, 0].reshape(fresh, HEAD), q, contract, preferred_element_type=F32)
        key = lax.broadcasted_iota(jnp.int32, (fresh, rows), 0)
        held = jnp.where(key < QTOK, me * QTOK, (me + 1 - 2 * core) * QTOK - QTOK)
        token = lax.broadcasted_iota(jnp.int32, (fresh, rows), 1) // GROUP
        live = key + held <= jnp.where(start == 0, token + b * QTOK, -1)
        new = jnp.where(live, new, NEG_FILL)
        top = jnp.max(new, axis=0, keepdims=True)
        scores, values = [], []
        for i in range(n):
            at = start + i
            mine = slots_ref[0, jnp.minimum(at, MOST - 1), b]
            theirs = slots_ref[1, jnp.clip(at - own, 0, MOST - 1), b]
            side = jnp.where(at < own, 0, 1)
            page = jnp.where(at < own, mine, theirs)
            score = lax.dot_general(k_ref[side, page], q, contract, preferred_element_type=F32)
            scores.append(score)
            values.append(vt_ref[side, page])
            most = jnp.max(score, axis=0, keepdims=True)
            top = jnp.maximum(top, jnp.where(i < live_pages, most, NEG_FILL))
        top = (top * FACTOR).astype(BF16).astype(F32)
        weights = jnp.where(live, jnp.exp2(new * FACTOR - top), 0.0).astype(BF16)
        both = jnp.dot(nvt[...], weights, preferred_element_type=F32)
        if n:
            weights = [
                jnp.exp2(s * FACTOR - jnp.where(i < live_pages, top, -NEG_FILL)).astype(BF16)
                for i, s in enumerate(scores)
            ]
            both = both + jnp.dot(
                jnp.concatenate(values, axis=1), jnp.concatenate(weights, axis=0), preferred_element_type=F32
            )
        return top, both

    def pair(i, _):
        slots = 2 * i, 2 * i + 1
        counts = [counts_ref[0, 0, block_of(s)] + counts_ref[1, 0, block_of(s)] for s in slots]
        most = jnp.maximum(counts[0], counts[1])

        def turn(r, _):
            start = r * MOST

            @pl.when(r > 0)
            def _():
                earlier[...] = out_ref[pl.ds(2 * i, 2)]

            steps = (jnp.minimum(most - start, MOST) + 1) // 2

            def case(n):
                def run():
                    for slot, (top, both) in [(s, attend(s, n, start)) for s in slots]:
                        for half in HALVES:
                            cols = slice(half * HALF, (half + 1) * HALF)
                            write_message(
                                out_ref.at[slot, half], top[:, cols], both[HEAD : HEAD + 1, cols], both[0:HEAD, cols]
                            )

                return run

            for n in range(0, MOST + 1, 2):
                pl.when(steps == n // 2)(case(n))

            @pl.when(r > 0)
            def _():
                for j, slot in enumerate(slots):
                    for half in HALVES:
                        whole = merged([out_ref.at[slot, half], earlier.at[j, half]])
                        write_message(out_ref.at[slot, half], *whole)

            return 0

        lax.fori_loop(0, jnp.where(most > MOST, 2, 1), turn, 0)
        return 0

    lax.fori_loop(0, COLUMN // 2, pair, 0)


def partials(slots, counts, q, k, vt, new):
    return pl.pallas_call(
        partial_kernel,
        out_shape=jax.ShapeDtypeStruct((COLUMN, 2, MSG, HALF), BF16),
        in_specs=[pl.BlockSpec(memory_space=pltpu.SMEM)] * 2 + [pl.BlockSpec(memory_space=pltpu.VMEM)] * 4,
        out_specs=pl.BlockSpec(memory_space=pltpu.VMEM),
        scratch_shapes=[pltpu.VMEM((MSG, 2 * QTOK), BF16), pltpu.VMEM((2, 2, MSG, HALF), BF16)],
        compiler_params=pltpu.CompilerParams(vmem_limit_bytes=24 * MIB),
        name="partials",
    )(slots, counts, q, k, vt, new)


def finish_kernel(
    p_ref, w_ref, out_ref,
    t_buf, r_buf, y_buf, turned, a_buf, mine_buf, kv_buf,
    rz_send, rz_recv, ry_send, ry_recv, kv_send, kv_recv, *sems,
):
    place = Place()
    peers = [dict(ctx=where) for where in (place.above, place.below, place.partner, place.sibling)]
    for off in range(1, ZS):
        other = lax.rem(place.kv + off, ZS)
        peers += [dict(kv=other), dict(ctx=place.sibling, kv=other)]
    greet(peers)
    started = []

    def begin(copy):
        copy.start()
        started.append(copy)

    def mine(dz, chain, half):
        return p_ref.at[place.slot(dz, chain), half]

    def z_copy(chain, way, step, half):
        at = chain, way, step - 1, half
        src = mine(WAYS[way] * LEN[chain][1 - way], chain, half) if step == 1 else t_buf.at[at]
        return remote(src, r_buf.at[at], rz_send.at[at], rz_recv.at[at], ctx=place.along(way))

    for step in range(1, 5):
        for chain in (1, 0):
            for half in HALVES:
                for way in (0, 1):
                    length = LEN[chain][1 - way]
                    if step > length:
                        continue
                    if step > 1:
                        z_copy(chain, way, step - 1, half).wait_recv()
                        parts = [
                            mine(WAYS[way] * (length + 1 - step), chain, half),
                            r_buf.at[chain, way, step - 2, half],
                        ]
                        write_message(t_buf.at[chain, way, step - 1, half], *merged(parts))
                    begin(z_copy(chain, way, step, half))

    def home(chain, half):
        parts = [mine(0, chain, half)]
        for way in (0, 1):
            length = LEN[chain][1 - way]
            z_copy(chain, way, length, half).wait_recv()
            parts.append(r_buf.at[chain, way, length - 1, half])
        return parts

    def y_copy(half):
        return remote(
            y_buf.at[0, half], y_buf.at[1, half], ry_send.at[half], ry_recv.at[half], ctx=place.partner
        )

    for half in HALVES:
        write_message(y_buf.at[0, half], *merged(home(1, half)))
        begin(y_copy(half))

    here = place.slot(0, 0)
    gather = Gather(place, a_buf, lambda half: a_buf.at[here, half], *sems)
    for half in HALVES:
        parts = home(0, half)
        y_copy(half).wait_recv()
        _, total, sums = merged(parts + [y_buf.at[1, half]])
        turned[half] = (sums * (1.0 / total)).T
        tokens = QTOK // 2
        for g in range(GROUP):
            a_buf[here, half, :, g * HEAD : (g + 1) * HEAD] = turned[
                half, pl.ds(g, tokens, stride=GROUP), :
            ].astype(BF16)
        gather.start(half)

    width = w_ref.shape[2]

    def project(dz):
        plane = lax.rem(place.z + dz + ZS, ZS)
        rows = a_buf[pl.ds(plane * 2, 2)].reshape(2 * QTOK, a_buf.shape[3])
        for side in (0, 1):
            done = jnp.dot(rows, w_ref[side], preferred_element_type=F32)
            mine_buf[plane, side] = done.astype(BF16)

        def copy(side, **where):
            return remote(
                mine_buf.at[plane, side], kv_buf.at[place.kv, side],
                kv_send.at[plane, side], kv_recv.at[place.kv, side], **where,
            )

        @pl.when(plane != place.kv)
        def _():
            copy(0, kv=plane).start()
            copy(1, ctx=place.sibling, kv=plane).start()

        @pl.when(plane == place.kv)
        def _():
            copy(1, ctx=place.sibling).start()

    gather.hop(0, 1)
    gather.partner()
    gather.hop(0, 2)
    project(0)
    gather.hop(1, 1)
    gather.hop(0, 3)
    project(1)
    project(-1)
    gather.hop(1, 2)
    gather.hop(0, 4)
    project(2)
    project(-2)
    gather.hop(1, 3)
    project(3)
    project(-3)
    gather.hop(1, 4)
    project(4)

    totals = [mine_buf[place.kv, 0].astype(F32), None]
    for off in range(ZS):
        other = lax.rem(place.kv + off, ZS)
        for side in (0, 1):
            if off == 0 and side == 0:
                continue
            where = dict(kv=other) if side == 0 else dict(ctx=place.sibling, kv=other)
            remote(
                mine_buf.at[other, side], kv_buf.at[other, side],
                kv_send.at[other, side], kv_recv.at[other, side], **where,
            ).wait()
            piece = kv_buf[other, side].astype(F32)
            totals[side] = piece if totals[side] is None else totals[side] + piece
    for side in (0, 1):
        core = place.core if side == 0 else 1 - place.core
        done = totals[side].astype(BF16).reshape(2, QTOK, width)
        for yh in (0, 1):
            out_ref[pl.ds(pl.multiple_of(yh * 2 * QTOK + core * QTOK, QTOK), QTOK), :] = done[yh]
    for copy in started:
        copy.wait_send()
    gather.finish()


def finish(p, w):
    depth, width = w.shape[1:]
    return pl.pallas_call(
        finish_kernel,
        out_shape=jax.ShapeDtypeStruct((4 * QTOK, width), BF16),
        in_specs=[pl.BlockSpec(memory_space=pltpu.VMEM)] * 2,
        out_specs=pl.BlockSpec(memory_space=pltpu.VMEM),
        scratch_shapes=[
            pltpu.VMEM((2, 2, 4, 2, MSG, HALF), BF16),
            pltpu.VMEM((2, 2, 4, 2, MSG, HALF), BF16),
            pltpu.VMEM((2, 2, MSG, HALF), BF16),
            pltpu.VMEM((2, HALF, HEAD), F32),
            pltpu.VMEM((COLUMN, 2, QTOK // 2, depth), BF16),
            pltpu.VMEM((ZS, 2, 2 * QTOK, width), BF16),
            pltpu.VMEM((ZS, 2, 2 * QTOK, width), BF16),
            pltpu.SemaphoreType.DMA((2, 2, 4, 2)),
            pltpu.SemaphoreType.DMA((2, 2, 4, 2)),
            pltpu.SemaphoreType.DMA((2,)),
            pltpu.SemaphoreType.DMA((2,)),
            pltpu.SemaphoreType.DMA((ZS, 2)),
            pltpu.SemaphoreType.DMA((ZS, 2)),
        ]
        + GATHER_SEMS,
        compiler_params=pltpu.CompilerParams(
            collective_id=1, has_side_effects=True, vmem_limit_bytes=24 * MIB
        ),
        name="finish",
    )(p, w)


def body(queries, new_keys, new_values, key_cache, value_cache, page_slots, page_counts, out_weight):
    q = queries.reshape(2, HALF, HEAD)
    nk = new_keys.reshape(QTOK, HEAD)
    nv = new_values.reshape(QTOK, HEAD)
    k = key_cache.reshape(-1, PAGE, HEAD)
    v = value_cache.reshape(-1, PAGE, HEAD)
    arrays = q, k, v, nk, nv, page_slots[0].T, page_counts, out_weight
    q_all, k_all, vt_all, new_all, slots, counts, w_all = exchange(
        *(pltpu.with_memory_space_constraint(array, pltpu.HBM) for array in arrays)
    )
    p = partials(slots, counts, q_all, k_all, vt_all, new_all)
    return finish(p, w_all)


def solution(mesh):
    placed = (
        P("ctx", "kv", None),
        P("ctx", "kv", None),
        P("ctx", "kv", None),
        P("ctx", "kv", None),
        P("ctx", "kv", None),
        P("ctx", None, None),
        P("ctx", None),
        P("kv", "ctx"),
    )
    return jax.shard_map(
        body, mesh=mesh, in_specs=placed, out_specs=P("kv", "ctx"), check_vma=False
    )
```

time: 644 us -> 85.1 us (0.13); the launches traced: 633 us -> 85 us
  blocking collectives: 178 us -> 0 us
  local copies, waits for them, and re-layouts: 172 us -> 0.63 us
  waiting for transfers between devices: 117 us -> 0 us
  Pallas kernels: 0 us -> 84.4 us
  starting transfers between devices: 59.5 us -> 0 us
  matrix products: 48.3 us -> 0 us
  other arithmetic: 41.9 us -> 0 us
  between operations: 13.7 us -> 0.02 us
    all_gather x2 -> x0, blocking collectives: 165 us -> none  [the longest x1 125 us: body(): lax.all_gather(new_keys, 'ctx', axis=0, tiled=True)]
    gather x64 -> x0, local copies, waits for them, and re-layouts: 140 us -> none  [the longest x32 70.1 us: block_part(): jnp.take(key_pages, page_list, axis=0).reshape(-1, kv_local, width)]
    pallas_call x0 -> x3, Pallas kernels: none -> 84.4 us  [the longest x1 49.6 us: finish(): pl.pallas_call(finish_kernel, out_shape=jax.ShapeDtypeStruct((4 * QTOK, w...]
    all_gather x1 -> x0, waiting for transfers between devices: 79.7 us -> none  [body(): context = lax.all_gather(attention, 'ctx', axis=0, tiled=True)]
    dot_general x67 -> x0, matrix products: 48.3 us -> none  [the longest x33 31.9 us: masked_part(): jnp.einsum('tkgn,nkd->tkgd', weights, value_rows, preferred_element_type=...]
    ppermute x31 -> x0, starting transfers between devices: 45.9 us -> none  [from_behind(): return lax.ppermute(value, axis, pairs)]
    reduce_scatter x1 -> x0, waiting for transfers between devices: 28.2 us -> none  [body(): lax.psum_scatter(jnp.dot(context, out_weight, preferred_element_type=jnp....]
    dynamic_slice x33 -> x0, local copies, waits for them, and re-layouts: 23 us -> none  [the longest x32 22.1 us: block_part(): live_count = count_table[block_index]]
  transfers between devices with their start and end apart: 35 -> 0, of which waited for: 3 -> 0; matrix products, arithmetic and copies ran while one was open for 30% -> 0% of each run, Pallas kernels for 0% -> 0%
where the time goes in v2:
time: 85.1 us; the launch traced here: 85 us
  Pallas kernels  84.4 us (99%)
    pallas_call x1, Pallas kernels, finish(): pl.pallas_call(finish_kernel, out_shape=jax.ShapeDtypeStruct((4 * QTOK, w...  49.6 us
    pallas_call x1, Pallas kernels, exchange(): pl.pallas_call(exchange_kernel, out_shape=(jax.ShapeDtypeStruct((COLUMN,...  23.4 us
    pallas_call x1, Pallas kernels, partials(): pl.pallas_call(partial_kernel, out_shape=jax.ShapeDtypeStruct((COLUMN, 2,...  11.4 us

profile of v2, /device:TPU:5, one launch (start us, length us, event | category | flops | bytes accessed | tf_op | source)
XLA Modules:
  0.0 85.0 jit_solution(11550838846324075854)
XLA Ops:
  0.0 23.4 %exchange.1 = (bf16[16,2,128,128]{3,2,1,0:T(8,128)(2,1)S(1)}, bf16[2,64,128,128]{3,2,1,0:T(8,128)(2,1)S(1)}, bf16[2,64,144,128]{3,2,1,0:T(8,128)(2,1)S(1)}, bf16...) custom-call(bf16[2,128,128]{2,1,0:T(8,128)(2,1)} %bitcast.10, ...), custom_call_target="tpu_custom_call" | custom-call | tf_op jit(solution)/shard_map/exchange/pallas_call | solution.py:222
  23.4 11.4 %partials.1.p_ref = bf16[16,2,144,128]{3,2,1,0:T(8,128)(2,1)S(1)} custom-call(s32[2,8,32]{2,1,0:T(8,128)S(1)} %get-tuple-element.12.slots_ref, s32[2,1,32]{2,1,0:T(1,128)S(1)} %get-tuple-element.13.counts_ref, bf16[16,2,128,128]{3,2,1,0:T(8,128)(2,1)S(1)} %get-tuple-element.14.q_ref, bf16[2,64,128,128]{3,2,1,0:T(8,128)(2,1)S(1)} %get-tuple-element.15.k_ref, ...), custom_call_target="tpu_custom_call" | custom-call | tf_op jit(solution)/shard_map/partials/pallas_call | solution.py:371
  34.7 49.6 %finish.1 = bf16[128,256]{1,0:T(8,128)(2,1)S(1)} custom-call(bf16[16,2,144,128]{3,2,1,0:T(8,128)(2,1)S(1)} %partials.1.p_ref, bf16[2,1024,256]{2,1,0:T(8,128)(2,1)S(1)} %get-tuple-element.18.w_ref), custom_call_target="tpu_custom_call" | custom-call | tf_op jit(solution)/shard_map/finish/pallas_call | solution.py:521
  84.4 0.6 copy.10

commit v3 on v2

--- a/solution.py
+++ b/solution.py
@@ -14,6 +14,7 @@
 ZS = 8
 COLUMN = 16
 MOST = 8
+TEAM = 4
 NEG_FILL = -1e30
 FACTOR = HEAD ** (-0.5) * 1.4426950408889634
 MIB = 1 << 20
@@ -21,9 +22,9 @@
 BF16 = jnp.bfloat16
 F32 = jnp.float32
 
-LEN = ((4, 3), (3, 4))
 WAYS = (1, -1)
 HALVES = (0, 1)
+FAR = 4
 
 
 class Place:
@@ -33,10 +34,12 @@
         self.z = self.me // 4
         self.yh = (self.me % 4) // 2
         self.core = self.me % 2
-        self.above = self.block(1, 0)
-        self.below = self.block(-1, 0)
         self.partner = self.block(0, 1)
         self.sibling = self.z * 4 + self.yh * 2 + 1 - self.core
+        self.first = jnp.where(self.z % 4 < 2, 1, 0)
+
+    def neighbours(self):
+        return [self.block(dz, chain) for chain in (0, 1) for dz in WAYS] + [self.partner, self.sibling]
 
     def slot(self, dz, chain):
         z = lax.rem(self.z + dz + ZS, ZS)
@@ -45,8 +48,8 @@
     def block(self, dz, chain):
         return self.slot(dz, chain) * 2 + self.core
 
-    def along(self, way):
-        return self.below if way else self.above
+    def ways(self):
+        return self.first, 1 - self.first
 
 
 def remote(src, dst, send, recv, **where):
@@ -62,63 +65,71 @@
     pl.semaphore_wait(barrier, len(wheres))
 
 
+def sign(way):
+    return 1 - 2 * way
+
+
 class Gather:
     def __init__(self, place, slots, own, z_send, z_recv, y_send, y_recv):
         self.place, self.slots, self.own = place, slots, own
-        self.sems = z_send, z_recv, y_send, y_recv
-        self.started = []
-
-    def z_copy(self, chain, way, step, half, src=None):
-        here = self.slots.at[self.place.slot(-(step - 1) * WAYS[way], chain), half]
+        self.z_send, self.z_recv, self.y_send, self.y_recv = z_send, z_recv, y_send, y_recv
+
+    def hop_to(self, chain, way, step, half):
         at = chain, way, step - 1, half
-        return remote(
-            here if src is None else src, here, self.sems[0].at[at], self.sems[1].at[at], ctx=self.place.along(way)
-        )
-
-    def z_start(self, *args, **more):
-        copy = self.z_copy(*args, **more)
-        copy.start()
-        self.started.append(copy)
-
-    def z_wait(self, chain, way, step, half):
-        there = self.slots.at[self.place.slot(-step * WAYS[way], chain), half]
+        if step == 1:
+            src, dst = self.own(half), self.slots.at[self.place.slot(0, 0), half]
+        else:
+            src = dst = self.slots.at[self.place.slot((1 - step) * sign(way), chain), half]
+        target = self.place.block(sign(way), chain if step == 1 else 0)
+        return remote(src, dst, self.z_send.at[at], self.z_recv.at[at], ctx=target)
+
+    def hop_from(self, chain, way, step, half):
         at = chain, way, step - 1, half
-        remote(there, there, self.sems[0].at[at], self.sems[1].at[at], ctx=self.place.along(way)).wait_recv()
+        there = self.slots.at[self.place.slot(-step * sign(way), chain), half]
+        return remote(there, there, self.z_send.at[at], self.z_recv.at[at], ctx=self.place.partner)
+
+    def across(self, half):
+        dst = self.slots.at[self.place.slot(0, 0), half]
+        return remote(self.own(half), dst, self.y_send.at[half], self.y_recv.at[half], ctx=self.place.partner)
 
     def start(self, half):
-        src = self.own(half)
-        copy = remote(
-            src, self.slots.at[self.place.slot(0, 0), half], self.sems[2].at[half], self.sems[3].at[half],
-            ctx=self.place.partner,
-        )
-        copy.start()
-        self.started.append(copy)
-        for way in (0, 1):
-            self.z_start(0, way, 1, half, src=src)
-
-    def partner(self):
+        for chain in (0, 1):
+            for way in (0, 1):
+                self.hop_to(chain, way, 1, half).start()
+
+    def start_across(self):
+        for half in HALVES:
+            self.across(half).start()
+
+    def wait_across(self):
         for half in HALVES:
             there = self.slots.at[self.place.slot(0, 1), half]
             remote(
-                there, there, self.sems[2].at[half], self.sems[3].at[half], ctx=self.place.partner
+                there, there, self.y_send.at[half], self.y_recv.at[half], ctx=self.place.partner
             ).wait_recv()
-            for way in (0, 1):
-                self.z_start(1, way, 1, half)
 
     def hop(self, chain, step, between=None):
         for half in HALVES:
-            for way in (0, 1):
-                if LEN[chain][way] < step:
-                    continue
-                if between is not None:
-                    between()
-                self.z_wait(chain, way, step, half)
-                if step < LEN[chain][way]:
-                    self.z_start(chain, way, step + 1, half)
+            if between is not None:
+                between()
+            if step == FAR:
+                self.hop_from(chain, half, step, half).wait_recv()
+                continue
+            for way in self.place.ways():
+                self.hop_from(chain, way, step, half).wait_recv()
+                onward = self.hop_to(chain, way, step + 1, half)
+                if step + 1 < FAR:
+                    onward.start()
+                else:
+                    pl.when(way == half)(onward.start)
 
     def finish(self):
-        for copy in self.started:
-            copy.wait_send()
+        for half in HALVES:
+            self.across(half).wait_send()
+            for chain in (0, 1):
+                for step in range(1, FAR + 1):
+                    for way in (0, 1) if step < FAR else (half,):
+                        self.hop_to(chain, way, step, half).wait_send()
 
 
 GATHER_SEMS = [
@@ -153,11 +164,12 @@
     ]
     for copy in local:
         copy.start()
-    greet([dict(ctx=where) for where in (place.above, place.below, place.partner, place.sibling)])
+    greet([dict(ctx=where) for where in place.neighbours()])
 
     gather = Gather(place, g_out, lambda half: q_ref.at[half], *sems)
     for half in HALVES:
         gather.start(half)
+    gather.start_across()
 
     to_sibling = []
 
@@ -177,8 +189,8 @@
         give(k_ref.at[part], k_out.at[1, part])
     give(w_ref, w_out.at[1])
 
-    todo = list(range(16))
-    each = pages // 16
+    todo = list(range(8))
+    each = pages // 8
 
     def between():
         if not todo:
@@ -194,21 +206,18 @@
             return 0
 
         lax.fori_loop(i * each, (i + 1) * each, turn, 0)
-        if i % 4 == 3:
-            part = pl.ds((i - 3) * each, 4 * each), pl.ds(0, HEAD)
+        if i % 2 == 1:
+            part = pl.ds((i - 1) * each, 2 * each), pl.ds(0, HEAD)
             give(vt_out.at[(0,) + part], vt_out.at[(1,) + part])
 
-    gather.hop(0, 1, between)
-    gather.partner()
-    gather.hop(0, 2, between)
-    gather.hop(1, 1, between)
-    gather.hop(0, 3, between)
-    gather.hop(1, 2, between)
+    for step in range(1, FAR):
+        for chain in (0, 1):
+            gather.hop(chain, step, between)
     while todo:
         between()
-    gather.hop(0, 4)
-    gather.hop(1, 3)
-    gather.hop(1, 4)
+    for chain in (0, 1):
+        gather.hop(chain, FAR)
+    gather.wait_across()
     gather.finish()
     for copy in local[1:]:
         copy.wait()
@@ -274,29 +283,37 @@
     return top, total, sums
 
 
-def partial_kernel(slots_ref, counts_ref, q_ref, k_ref, vt_ref, new_ref, out_ref, nvt, earlier):
+def partial_kernel(
+    slots_ref, counts_ref, q_ref, k_ref, vt_ref, new_ref, out_ref, nvt, lag, earlier, count_of, order
+):
     me = lax.axis_index("ctx")
     core = me % 2
-    pages = k_ref.shape[1]
     contract = (((1,), (1,)), ((), ()))
     fresh = 2 * QTOK
     rows = 2 * HALF
     nvt[0:HEAD, :] = new_ref[:, 1].reshape(fresh, HEAD).astype(F32).T.astype(BF16)
     nvt[HEAD:MSG, :] = jnp.ones((MSG - HEAD, fresh), BF16)
-
-    def block_of(slot):
-        return slot * 2 + core
+    key = lax.broadcasted_iota(jnp.int32, (fresh, rows), 0)
+    held = jnp.where(key < QTOK, me * QTOK, (me - 2 * core) * QTOK)
+    lag[...] = key + held - lax.broadcasted_iota(jnp.int32, (fresh, rows), 1) // GROUP
+
+    counts = [counts_ref[0, 0, 2 * j + core] + counts_ref[1, 0, 2 * j + core] for j in range(COLUMN)]
+    for j in range(COLUMN):
+        rank = 0
+        for i in range(COLUMN):
+            if i != j:
+                ahead = counts[i] >= counts[j] if i < j else counts[i] > counts[j]
+                rank = rank + ahead.astype(jnp.int32)
+        order[rank] = j
+        count_of[j] = counts[j]
 
     def attend(slot, n, start):
-        b = block_of(slot)
+        b = slot * 2 + core
         own = counts_ref[0, 0, b]
-        live_pages = own + counts_ref[1, 0, b] - start
+        live_pages = count_of[slot] - start
         q = q_ref[slot].reshape(rows, HEAD)
         new = lax.dot_general(new_ref[:, 0].reshape(fresh, HEAD), q, contract, preferred_element_type=F32)
-        key = lax.broadcasted_iota(jnp.int32, (fresh, rows), 0)
-        held = jnp.where(key < QTOK, me * QTOK, (me + 1 - 2 * core) * QTOK - QTOK)
-        token = lax.broadcasted_iota(jnp.int32, (fresh, rows), 1) // GROUP
-        live = key + held <= jnp.where(start == 0, token + b * QTOK, -1)
+        live = lag[...] <= jnp.where(start == 0, b * QTOK, -2 * COLUMN * QTOK)
         new = jnp.where(live, new, NEG_FILL)
         top = jnp.max(new, axis=0, keepdims=True)
         scores, values = [], []
@@ -324,17 +341,17 @@
             )
         return top, both
 
-    def pair(i, _):
-        slots = 2 * i, 2 * i + 1
-        counts = [counts_ref[0, 0, block_of(s)] + counts_ref[1, 0, block_of(s)] for s in slots]
-        most = jnp.maximum(counts[0], counts[1])
+    def team(i, _):
+        slots = [order[i * TEAM + j] for j in range(TEAM)]
+        most = count_of[slots[0]]
 
         def turn(r, _):
             start = r * MOST
 
             @pl.when(r > 0)
             def _():
-                earlier[...] = out_ref[pl.ds(2 * i, 2)]
+                for j, slot in enumerate(slots):
+                    earlier[j] = out_ref[slot]
 
             steps = (jnp.minimum(most - start, MOST) + 1) // 2
 
@@ -364,7 +381,7 @@
         lax.fori_loop(0, jnp.where(most > MOST, 2, 1), turn, 0)
         return 0
 
-    lax.fori_loop(0, COLUMN // 2, pair, 0)
+    lax.fori_loop(0, COLUMN // TEAM, team, 0)
 
 
 def partials(slots, counts, q, k, vt, new):
@@ -373,7 +390,13 @@
         out_shape=jax.ShapeDtypeStruct((COLUMN, 2, MSG, HALF), BF16),
         in_specs=[pl.BlockSpec(memory_space=pltpu.SMEM)] * 2 + [pl.BlockSpec(memory_space=pltpu.VMEM)] * 4,
         out_specs=pl.BlockSpec(memory_space=pltpu.VMEM),
-        scratch_shapes=[pltpu.VMEM((MSG, 2 * QTOK), BF16), pltpu.VMEM((2, 2, MSG, HALF), BF16)],
+        scratch_shapes=[
+            pltpu.VMEM((MSG, 2 * QTOK), BF16),
+            pltpu.VMEM((2 * QTOK, 2 * HALF), jnp.int32),
+            pltpu.VMEM((TEAM, 2, MSG, HALF), BF16),
+            pltpu.SMEM((COLUMN,), jnp.int32),
+            pltpu.SMEM((COLUMN,), jnp.int32),
+        ],
         compiler_params=pltpu.CompilerParams(vmem_limit_bytes=24 * MIB),
         name="partials",
     )(slots, counts, q, k, vt, new)
@@ -385,64 +408,63 @@
     rz_send, rz_recv, ry_send, ry_recv, kv_send, kv_recv, *sems,
 ):
     place = Place()
-    peers = [dict(ctx=where) for where in (place.above, place.below, place.partner, place.sibling)]
+    peers = [dict(ctx=where) for where in place.neighbours()]
     for off in range(1, ZS):
         other = lax.rem(place.kv + off, ZS)
         peers += [dict(kv=other), dict(ctx=place.sibling, kv=other)]
     greet(peers)
-    started = []
-
-    def begin(copy):
-        copy.start()
-        started.append(copy)
 
     def mine(dz, chain, half):
         return p_ref.at[place.slot(dz, chain), half]
 
-    def z_copy(chain, way, step, half):
-        at = chain, way, step - 1, half
-        src = mine(WAYS[way] * LEN[chain][1 - way], chain, half) if step == 1 else t_buf.at[at]
-        return remote(src, r_buf.at[at], rz_send.at[at], rz_recv.at[at], ctx=place.along(way))
-
-    for step in range(1, 5):
-        for chain in (1, 0):
-            for half in HALVES:
-                for way in (0, 1):
-                    length = LEN[chain][1 - way]
-                    if step > length:
-                        continue
-                    if step > 1:
-                        z_copy(chain, way, step - 1, half).wait_recv()
-                        parts = [
-                            mine(WAYS[way] * (length + 1 - step), chain, half),
-                            r_buf.at[chain, way, step - 2, half],
-                        ]
-                        write_message(t_buf.at[chain, way, step - 1, half], *merged(parts))
-                    begin(z_copy(chain, way, step, half))
-
-    def home(chain, half):
-        parts = [mine(0, chain, half)]
-        for way in (0, 1):
-            length = LEN[chain][1 - way]
-            z_copy(chain, way, length, half).wait_recv()
-            parts.append(r_buf.at[chain, way, length - 1, half])
-        return parts
+    def fold_to(chain, way, left, half):
+        at = chain, way, left - 1, half
+        entry = left == FAR or (left == FAR - 1 and isinstance(way, int) and way != half)
+        src = mine(sign(way) * left, chain, half) if entry else t_buf.at[at]
+        target = place.block(sign(way), chain if left == 1 else 0)
+        return remote(src, r_buf.at[at], rz_send.at[at], rz_recv.at[at], ctx=target)
+
+    def fold_from(chain, way, left, half):
+        at = chain, way, left - 1, half
+        remote(r_buf.at[at], r_buf.at[at], rz_send.at[at], rz_recv.at[at], ctx=place.partner).wait_recv()
+        return r_buf.at[at]
+
+    def fold(chain, way, left, half):
+        parts = [mine(sign(way) * left, chain, half), fold_from(chain, way, left + 1, half)]
+        write_message(t_buf.at[chain, way, left - 1, half], *merged(parts))
+        fold_to(chain, way, left, half).start()
 
     def y_copy(half):
         return remote(
-            y_buf.at[0, half], y_buf.at[1, half], ry_send.at[half], ry_recv.at[half], ctx=place.partner
+            mine(0, 1, half), y_buf.at[half], ry_send.at[half], ry_recv.at[half], ctx=place.partner
         )
 
     for half in HALVES:
-        write_message(y_buf.at[0, half], *merged(home(1, half)))
-        begin(y_copy(half))
+        for chain in (1, 0):
+            fold_to(chain, half, FAR, half).start()
+    for half in HALVES:
+        for chain in (1, 0):
+            fold_to(chain, 1 - half, FAR - 1, half).start()
+    for half in HALVES:
+        y_copy(half).start()
+    for half in HALVES:
+        for chain in (1, 0):
+            fold(chain, half, FAR - 1, half)
+    for left in (2, 1):
+        for half in HALVES:
+            for chain in (1, 0):
+                for way in place.ways():
+                    fold(chain, way, left, half)
 
     here = place.slot(0, 0)
     gather = Gather(place, a_buf, lambda half: a_buf.at[here, half], *sems)
     for half in HALVES:
-        parts = home(0, half)
-        y_copy(half).wait_recv()
-        _, total, sums = merged(parts + [y_buf.at[1, half]])
+        parts = [mine(0, 0, half)]
+        for chain in (1, 0):
+            for way in (0, 1):
+                parts.append(fold_from(chain, way, 1, half))
+        remote(y_buf.at[half], y_buf.at[half], ry_send.at[half], ry_recv.at[half], ctx=place.partner).wait_recv()
+        _, total, sums = merged(parts + [y_buf.at[half]])
         turned[half] = (sums * (1.0 / total)).T
         tokens = QTOK // 2
         for g in range(GROUP):
@@ -450,6 +472,7 @@
                 half, pl.ds(g, tokens, stride=GROUP), :
             ].astype(BF16)
         gather.start(half)
+    gather.start_across()
 
     width = w_ref.shape[2]
 
@@ -475,23 +498,20 @@
         def _():
             copy(1, ctx=place.sibling).start()
 
-    gather.hop(0, 1)
-    gather.partner()
-    gather.hop(0, 2)
-    project(0)
-    gather.hop(1, 1)
-    gather.hop(0, 3)
-    project(1)
-    project(-1)
-    gather.hop(1, 2)
-    gather.hop(0, 4)
-    project(2)
-    project(-2)
-    gather.hop(1, 3)
-    project(3)
-    project(-3)
-    gather.hop(1, 4)
-    project(4)
+    for step in range(1, FAR):
+        for chain in (0, 1):
+            gather.hop(chain, step)
+        if step == 1:
+            gather.wait_across()
+            project(0)
+        else:
+            project(step - 1)
+            project(1 - step)
+    project(FAR - 1)
+    project(1 - FAR)
+    for chain in (0, 1):
+        gather.hop(chain, FAR)
+    project(FAR)
 
     totals = [mine_buf[place.kv, 0].astype(F32), None]
     for off in range(ZS):
@@ -511,8 +531,12 @@
         done = totals[side].astype(BF16).reshape(2, QTOK, width)
         for yh in (0, 1):
             out_ref[pl.ds(pl.multiple_of(yh * 2 * QTOK + core * QTOK, QTOK), QTOK), :] = done[yh]
-    for copy in started:
-        copy.wait_send()
+    for half in HALVES:
+        y_copy(half).wait_send()
+        for chain in (0, 1):
+            for left in range(1, FAR + 1):
+                for way in (0, 1) if left < FAR else (half,):
+                    fold_to(chain, way, left, half).wait_send()
     gather.finish()
 
 
@@ -526,7 +550,7 @@
         scratch_shapes=[
             pltpu.VMEM((2, 2, 4, 2, MSG, HALF), BF16),
             pltpu.VMEM((2, 2, 4, 2, MSG, HALF), BF16),
-            pltpu.VMEM((2, 2, MSG, HALF), BF16),
+            pltpu.VMEM((2, MSG, HALF), BF16),
             pltpu.VMEM((2, HALF, HEAD), F32),
             pltpu.VMEM((COLUMN, 2, QTOK // 2, depth), BF16),
             pltpu.VMEM((ZS, 2, 2 * QTOK, width), BF16),

time: 85.1 us -> 77.3 us (0.908)
  Pallas kernels: 84.4 us -> 76.6 us
    pallas_call x1, Pallas kernels: 11.4 us -> 8.09 us  [partials(): pl.pallas_call(partial_kernel, out_shape=jax.ShapeDtypeStruct((COLUMN, 2,...]
    pallas_call x1, Pallas kernels: 49.6 us -> 46.7 us  [finish(): pl.pallas_call(finish_kernel, out_shape=jax.ShapeDtypeStruct((4 * QTOK, w...]
    pallas_call x1, Pallas kernels: 23.4 us -> 21.8 us  [exchange(): pl.pallas_call(exchange_kernel, out_shape=(jax.ShapeDtypeStruct((COLUMN,...]
where the time goes in v3:
time: 77.3 us; the launch traced here: 77.2 us
  Pallas kernels  76.6 us (99%)
    pallas_call x1, Pallas kernels, finish(): pl.pallas_call(finish_kernel, out_shape=jax.ShapeDtypeStruct((4 * QTOK, w...  46.7 us
    pallas_call x1, Pallas kernels, exchange(): pl.pallas_call(exchange_kernel, out_shape=(jax.ShapeDtypeStruct((COLUMN,...  21.8 us
    pallas_call x1, Pallas kernels, partials(): pl.pallas_call(partial_kernel, out_shape=jax.ShapeDtypeStruct((COLUMN, 2,...  8.09 us

profile of v3, /device:TPU:5, one launch (start us, length us, event | category | flops | bytes accessed | tf_op | source)
XLA Modules:
  0.0 77.2 jit_solution(3033328521435680835)
XLA Ops:
  0.0 21.8 %exchange.1 = (bf16[16,2,128,128]{3,2,1,0:T(8,128)(2,1)S(1)}, bf16[2,64,128,128]{3,2,1,0:T(8,128)(2,1)S(1)}, bf16[2,64,144,128]{3,2,1,0:T(8,128)(2,1)S(1)}, bf16...) custom-call(bf16[2,128,128]{2,1,0:T(8,128)(2,1)} %bitcast.10, ...), custom_call_target="tpu_custom_call" | custom-call | tf_op jit(solution)/shard_map/exchange/pallas_call | solution.py:231
  21.8 8.1 %partials.1.p_ref = bf16[16,2,144,128]{3,2,1,0:T(8,128)(2,1)S(1)} custom-call(s32[2,8,32]{2,1,0:T(8,128)S(1)} %get-tuple-element.12.slots_ref, s32[2,1,32]{2,1,0:T(1,128)S(1)} %get-tuple-element.13.counts_ref, bf16[16,2,128,128]{3,2,1,0:T(8,128)(2,1)S(1)} %get-tuple-element.14.q_ref, bf16[2,64,128,128]{3,2,1,0:T(8,128)(2,1)S(1)} %get-tuple-element.15.k_ref, ...), custom_call_target="tpu_custom_call" | custom-call | tf_op jit(solution)/shard_map/partials/pallas_call | solution.py:388
  29.9 46.7 %finish.1 = bf16[128,256]{1,0:T(8,128)(2,1)S(1)} custom-call(bf16[16,2,144,128]{3,2,1,0:T(8,128)(2,1)S(1)} %partials.1.p_ref, bf16[2,1024,256]{2,1,0:T(8,128)(2,1)S(1)} %get-tuple-element.18.w_ref), custom_call_target="tpu_custom_call" | custom-call | tf_op jit(solution)/shard_map/finish/pallas_call | solution.py:545
  76.6 0.6 copy.10

commit v4 on v3

--- a/solution.py
+++ b/solution.py
@@ -25,6 +25,7 @@
 WAYS = (1, -1)
 HALVES = (0, 1)
 FAR = 4
+Q_PIECES = 2
 
 
 class Place:
@@ -39,7 +40,8 @@
         self.first = jnp.where(self.z % 4 < 2, 1, 0)
 
     def neighbours(self):
-        return [self.block(dz, chain) for chain in (0, 1) for dz in WAYS] + [self.partner, self.sibling]
+        near = [self.block(dz, chain) for chain in (0, 1) for dz in WAYS]
+        return near + [self.block(2 * dz, 0) for dz in WAYS] + [self.partner, self.sibling]
 
     def slot(self, dz, chain):
         z = lax.rem(self.z + dz + ZS, ZS)
@@ -70,74 +72,77 @@
 
 
 class Gather:
-    def __init__(self, place, slots, own, z_send, z_recv, y_send, y_recv):
-        self.place, self.slots, self.own = place, slots, own
+    def __init__(self, place, slots, own, leap, z_send, z_recv, y_send, y_recv):
+        self.place, self.slots, self.own, self.leap = place, slots, own, leap
         self.z_send, self.z_recv, self.y_send, self.y_recv = z_send, z_recv, y_send, y_recv
-
-    def hop_to(self, chain, way, step, half):
-        at = chain, way, step - 1, half
+        self.pieces = range(slots.shape[1])
+
+    def hop_to(self, chain, way, step, piece):
+        at = chain, way, step - 1, piece
+        jump = 2 if step == FAR and self.leap else 1
         if step == 1:
-            src, dst = self.own(half), self.slots.at[self.place.slot(0, 0), half]
+            src, dst = self.own(piece), self.slots.at[self.place.slot(0, 0), piece]
         else:
-            src = dst = self.slots.at[self.place.slot((1 - step) * sign(way), chain), half]
-        target = self.place.block(sign(way), chain if step == 1 else 0)
+            src = dst = self.slots.at[self.place.slot((jump - step) * sign(way), chain), piece]
+        target = self.place.block(jump * sign(way), chain if step == 1 else 0)
         return remote(src, dst, self.z_send.at[at], self.z_recv.at[at], ctx=target)
 
-    def hop_from(self, chain, way, step, half):
-        at = chain, way, step - 1, half
-        there = self.slots.at[self.place.slot(-step * sign(way), chain), half]
+    def hop_from(self, chain, way, step, piece):
+        at = chain, way, step - 1, piece
+        there = self.slots.at[self.place.slot(-step * sign(way), chain), piece]
         return remote(there, there, self.z_send.at[at], self.z_recv.at[at], ctx=self.place.partner)
 
-    def across(self, half):
-        dst = self.slots.at[self.place.slot(0, 0), half]
-        return remote(self.own(half), dst, self.y_send.at[half], self.y_recv.at[half], ctx=self.place.partner)
-
-    def start(self, half):
+    def across(self, piece):
+        dst = self.slots.at[self.place.slot(0, 0), piece]
+        return remote(self.own(piece), dst, self.y_send.at[piece], self.y_recv.at[piece], ctx=self.place.partner)
+
+    def start(self, piece):
         for chain in (0, 1):
             for way in (0, 1):
-                self.hop_to(chain, way, 1, half).start()
+                self.hop_to(chain, way, 1, piece).start()
 
     def start_across(self):
-        for half in HALVES:
-            self.across(half).start()
+        for piece in self.pieces:
+            self.across(piece).start()
 
     def wait_across(self):
-        for half in HALVES:
-            there = self.slots.at[self.place.slot(0, 1), half]
+        for piece in self.pieces:
+            there = self.slots.at[self.place.slot(0, 1), piece]
             remote(
-                there, there, self.y_send.at[half], self.y_recv.at[half], ctx=self.place.partner
+                there, there, self.y_send.at[piece], self.y_recv.at[piece], ctx=self.place.partner
             ).wait_recv()
 
     def hop(self, chain, step, between=None):
-        for half in HALVES:
+        for piece in self.pieces:
+            far = piece % 2
             if between is not None:
                 between()
             if step == FAR:
-                self.hop_from(chain, half, step, half).wait_recv()
+                self.hop_from(chain, far, step, piece).wait_recv()
                 continue
             for way in self.place.ways():
-                self.hop_from(chain, way, step, half).wait_recv()
-                onward = self.hop_to(chain, way, step + 1, half)
-                if step + 1 < FAR:
-                    onward.start()
-                else:
-                    pl.when(way == half)(onward.start)
+                self.hop_from(chain, way, step, piece).wait_recv()
+                if step == FAR - (2 if self.leap else 1):
+                    pl.when(way == far)(self.hop_to(chain, way, FAR, piece).start)
+                if step < FAR - 1:
+                    self.hop_to(chain, way, step + 1, piece).start()
 
     def finish(self):
-        for half in HALVES:
-            self.across(half).wait_send()
+        for piece in self.pieces:
+            self.across(piece).wait_send()
             for chain in (0, 1):
                 for step in range(1, FAR + 1):
-                    for way in (0, 1) if step < FAR else (half,):
-                        self.hop_to(chain, way, step, half).wait_send()
-
-
-GATHER_SEMS = [
-    pltpu.SemaphoreType.DMA((2, 2, 4, 2)),
-    pltpu.SemaphoreType.DMA((2, 2, 4, 2)),
-    pltpu.SemaphoreType.DMA((2,)),
-    pltpu.SemaphoreType.DMA((2,)),
-]
+                    for way in (0, 1) if step < FAR else (piece % 2,):
+                        self.hop_to(chain, way, step, piece).wait_send()
+
+
+def gather_sems(pieces):
+    return [
+        pltpu.SemaphoreType.DMA((2, 2, FAR, pieces)),
+        pltpu.SemaphoreType.DMA((2, 2, FAR, pieces)),
+        pltpu.SemaphoreType.DMA((pieces,)),
+        pltpu.SemaphoreType.DMA((pieces,)),
+    ]
 
 
 def exchange_kernel(
@@ -166,9 +171,9 @@
         copy.start()
     greet([dict(ctx=where) for where in place.neighbours()])
 
-    gather = Gather(place, g_out, lambda half: q_ref.at[half], *sems)
-    for half in HALVES:
-        gather.start(half)
+    gather = Gather(place, g_out, lambda piece: q_ref.at[piece], True, *sems)
+    for piece in gather.pieces:
+        gather.start(piece)
     gather.start_across()
 
     to_sibling = []
@@ -189,8 +194,8 @@
         give(k_ref.at[part], k_out.at[1, part])
     give(w_ref, w_out.at[1])
 
-    todo = list(range(8))
-    each = pages // 8
+    todo = list(range(16))
+    each = pages // 16
 
     def between():
         if not todo:
@@ -206,10 +211,12 @@
             return 0
 
         lax.fori_loop(i * each, (i + 1) * each, turn, 0)
-        if i % 2 == 1:
-            part = pl.ds((i - 1) * each, 2 * each), pl.ds(0, HEAD)
+        if i % 4 == 3:
+            part = pl.ds((i - 3) * each, 4 * each), pl.ds(0, HEAD)
             give(vt_out.at[(0,) + part], vt_out.at[(1,) + part])
 
+    for _ in range(8):
+        between()
     for step in range(1, FAR):
         for chain in (0, 1):
             gather.hop(chain, step, between)
@@ -231,7 +238,7 @@
     return pl.pallas_call(
         exchange_kernel,
         out_shape=(
-            jax.ShapeDtypeStruct((COLUMN, 2, HALF, HEAD), BF16),
+            jax.ShapeDtypeStruct((COLUMN,) + q.shape, BF16),
             jax.ShapeDtypeStruct((2, pages, PAGE, HEAD), BF16),
             jax.ShapeDtypeStruct((2, pages, MSG, PAGE), BF16),
             jax.ShapeDtypeStruct((2, 2, QTOK, HEAD), BF16),
@@ -247,7 +254,7 @@
             pltpu.SemaphoreType.DMA((n_give,)),
             pltpu.SemaphoreType.DMA((n_give,)),
         ]
-        + GATHER_SEMS,
+        + gather_sems(q.shape[0]),
         compiler_params=pltpu.CompilerParams(
             collective_id=0, has_side_effects=True, vmem_limit_bytes=24 * MIB
         ),
@@ -457,7 +464,7 @@
                     fold(chain, way, left, half)
 
     here = place.slot(0, 0)
-    gather = Gather(place, a_buf, lambda half: a_buf.at[here, half], *sems)
+    gather = Gather(place, a_buf, lambda half: a_buf.at[here, half], False, *sems)
     for half in HALVES:
         parts = [mine(0, 0, half)]
         for chain in (1, 0):
@@ -562,7 +569,7 @@
             pltpu.SemaphoreType.DMA((ZS, 2)),
             pltpu.SemaphoreType.DMA((ZS, 2)),
         ]
-        + GATHER_SEMS,
+        + gather_sems(2),
         compiler_params=pltpu.CompilerParams(
             collective_id=1, has_side_effects=True, vmem_limit_bytes=24 * MIB
         ),
@@ -571,7 +578,7 @@
 
 
 def body(queries, new_keys, new_values, key_cache, value_cache, page_slots, page_counts, out_weight):
-    q = queries.reshape(2, HALF, HEAD)
+    q = queries.reshape(Q_PIECES, 2 * HALF // Q_PIECES, HEAD)
     nk = new_keys.reshape(QTOK, HEAD)
     nv = new_values.reshape(QTOK, HEAD)
     k = key_cache.reshape(-1, PAGE, HEAD)

time: 77.3 us -> 76.3 us (0.987)
  Pallas kernels: 76.6 us -> 75.6 us
    pallas_call x1, Pallas kernels: 46.7 us -> 43.4 us  [finish(): pl.pallas_call(finish_kernel, out_shape=jax.ShapeDtypeStruct((4 * QTOK, w...]
    pallas_call x1, Pallas kernels: 8.09 us -> 10.2 us  [partials(): pl.pallas_call(partial_kernel, out_shape=jax.ShapeDtypeStruct((COLUMN, 2,...]
where the time goes in v4:
time: 76.3 us; the launch traced here: 76.2 us
  Pallas kernels  75.6 us (99%)
    pallas_call x1, Pallas kernels, finish(): pl.pallas_call(finish_kernel, out_shape=jax.ShapeDtypeStruct((4 * QTOK, w...  43.4 us
    pallas_call x1, Pallas kernels, exchange(): pl.pallas_call(exchange_kernel, out_shape=(jax.ShapeDtypeStruct((COLUMN,)...  21.9 us
    pallas_call x1, Pallas kernels, partials(): pl.pallas_call(partial_kernel, out_shape=jax.ShapeDtypeStruct((COLUMN, 2,...  10.2 us

profile of v4, /device:TPU:5, one launch (start us, length us, event | category | flops | bytes accessed | tf_op | source)
XLA Modules:
  0.0 76.2 jit_solution(9613962880859438492)
XLA Ops:
  0.0 21.9 %exchange.1 = (bf16[16,2,128,128]{3,2,1,0:T(8,128)(2,1)S(1)}, bf16[2,64,128,128]{3,2,1,0:T(8,128)(2,1)S(1)}, bf16[2,64,144,128]{3,2,1,0:T(8,128)(2,1)S(1)}, bf16...) custom-call(bf16[2,128,128]{2,1,0:T(8,128)(2,1)} %bitcast.10, ...), custom_call_target="tpu_custom_call" | custom-call | tf_op jit(solution)/shard_map/exchange/pallas_call | solution.py:238
  21.9 10.2 %partials.1.p_ref = bf16[16,2,144,128]{3,2,1,0:T(8,128)(2,1)S(1)} custom-call(s32[2,8,32]{2,1,0:T(8,128)S(1)} %get-tuple-element.12.slots_ref, s32[2,1,32]{2,1,0:T(1,128)S(1)} %get-tuple-element.13.counts_ref, bf16[16,2,128,128]{3,2,1,0:T(8,128)(2,1)S(1)} %get-tuple-element.14.q_ref, bf16[2,64,128,128]{3,2,1,0:T(8,128)(2,1)S(1)} %get-tuple-element.15.k_ref, ...), custom_call_target="tpu_custom_call" | custom-call | tf_op jit(solution)/shard_map/partials/pallas_call | solution.py:395
  32.2 43.4 %finish.1 = bf16[128,256]{1,0:T(8,128)(2,1)S(1)} custom-call(bf16[16,2,144,128]{3,2,1,0:T(8,128)(2,1)S(1)} %partials.1.p_ref, bf16[2,1024,256]{2,1,0:T(8,128)(2,1)S(1)} %get-tuple-element.18.w_ref), custom_call_target="tpu_custom_call" | custom-call | tf_op jit(solution)/shard_map/finish/pallas_call | solution.py:552
  75.6 0.6 copy.10
